TPU v7x, 128 devices: a whole 4x4x4 slice. The times are simulated.
128 devices in a mesh: narrow: 16 (over z, y_lo, core), wide: 8 (over y_hi, x).
Axes of the slice: x: 4, y: 4 (y_hi: 2, y_lo: 2; y = y_hi * 2 + y_lo), z: 4, core: 2. Of those that a mesh axis runs over, the one named last changes fastest.
Arguments:
- features: bfloat16 [4096, 16384], P(None, ('narrow', 'wide')), may hold values from -6 to 6
- in_proj: bfloat16 [768, 4096], P(('narrow', 'wide')), may hold values from -0.09375 to 0.09375
- short_taps: float32 [3, 768], replicated, may hold values from -3 to 3
- long_filter: bfloat16 [256, 16384], P(None, ('narrow', 'wide')), may hold values from -4 to 4
- out_grad: bfloat16 [256, 16384], P(None, ('narrow', 'wide')), may hold values from -11 to 11
Outputs:
- mixed_out: bfloat16 [256, 16384], P(None, ('narrow', 'wide'))
- feat_grad: bfloat16 [4096, 16384], P(None, ('narrow', 'wide'))
- filter_grad: bfloat16 [256, 16384], P(None, ('narrow', 'wide'))
- taps_grad: float32 [3, 768], replicated
- proj_grad: float32 [768, 4096], P(('narrow', 'wide'))
All inputs are finite; a program needn't handle non-finite values.
Results may differ from a plain program's by a relative error of at most 0.013.
Values may be sent and summed in bfloat16 or wider, within the bound.
A program may use at most 128 MiB of HBM per device.

v0:
```python
import math

import jax
import jax.numpy as jnp
from jax import lax
from jax.sharding import PartitionSpec as P

HIGH = lax.Precision.HIGHEST


def from_behind(value, axis, by):
    count = lax.axis_size(axis)
    pairs = [(i, i + by) for i in range(count) if 0 <= i + by < count]
    return lax.ppermute(value, axis, pairs)


def angles(count_a, count_b, period):
    left = jnp.arange(count_a, dtype=jnp.int32)[:, None]
    right = jnp.arange(count_b, dtype=jnp.int32)[None, :]
    phase = (left * right % period).astype(jnp.float32) * (2.0 * math.pi / period)
    return (jnp.cos(phase), jnp.sin(phase))


def make_tables(length):
    total = 2 * length
    power = total.bit_length() - 1
    rows_count = 2 ** (power // 2)
    cols_count = total // rows_count
    cos_r, sin_r = angles(rows_count, rows_count // 2, rows_count)
    cos_t, sin_t = angles(rows_count, cols_count, total)
    cos_m, sin_m = angles(cols_count, cols_count, cols_count)
    return (cos_r, sin_r, cos_t, sin_t, cos_m, sin_m, rows_count // 2, cols_count, total)


def forward_spectrum(signal, tables):
    cos_r, sin_r, cos_t, sin_t, cos_m, sin_m, half_rows, cols_count, total = tables
    grid = signal.reshape(signal.shape[0], half_rows, cols_count)
    real_a = jnp.einsum("fr,crm->cfm", cos_r, grid, precision=HIGH)
    imag_a = -jnp.einsum("fr,crm->cfm", sin_r, grid, precision=HIGH)
    real_b = real_a * cos_t + imag_a * sin_t
    imag_b = imag_a * cos_t - real_a * sin_t
    real_c = jnp.einsum("cfm,mk->cfk", real_b, cos_m, precision=HIGH) + jnp.einsum(
        "cfm,mk->cfk", imag_b, sin_m, precision=HIGH
    )
    imag_c = jnp.einsum("cfm,mk->cfk", imag_b, cos_m, precision=HIGH) - jnp.einsum(
        "cfm,mk->cfk", real_b, sin_m, precision=HIGH
    )
    return (real_c, imag_c)


def inverse_signal(real_s, imag_s, tables):
    cos_r, sin_r, cos_t, sin_t, cos_m, sin_m, half_rows, cols_count, total = tables
    real_c = jnp.einsum("cfk,km->cfm", real_s, cos_m, precision=HIGH) - jnp.einsum(
        "cfk,km->cfm", imag_s, sin_m, precision=HIGH
    )
    imag_c = jnp.einsum("cfk,km->cfm", imag_s, cos_m, precision=HIGH) + jnp.einsum(
        "cfk,km->cfm", real_s, sin_m, precision=HIGH
    )
    real_b = real_c * cos_t - imag_c * sin_t
    imag_b = imag_c * cos_t + real_c * sin_t
    grid = jnp.einsum("fr,cfm->crm", cos_r, real_b, precision=HIGH) - jnp.einsum(
        "fr,cfm->crm", sin_r, imag_b, precision=HIGH
    )
    grid = grid / float(total)
    return grid.reshape(grid.shape[0], half_rows * cols_count)


def convolve_channels(gated_ch, filter_ch, cot_ch):
    tables = make_tables(gated_ch.shape[1])
    gate_re, gate_im = forward_spectrum(gated_ch.astype(jnp.float32), tables)
    filt_re, filt_im = forward_spectrum(filter_ch.astype(jnp.float32), tables)
    cot_re, cot_im = forward_spectrum(cot_ch.astype(jnp.float32), tables)
    convolved = inverse_signal(
        filt_re * gate_re - filt_im * gate_im, filt_re * gate_im + filt_im * gate_re, tables
    )
    gate_grad = inverse_signal(
        filt_re * cot_re + filt_im * cot_im, filt_re * cot_im - filt_im * cot_re, tables
    )
    filter_grad = inverse_signal(
        gate_re * cot_re + gate_im * cot_im, gate_re * cot_im - gate_im * cot_re, tables
    )
    return (
        convolved.astype(jnp.bfloat16),
        gate_grad.astype(jnp.bfloat16),
        filter_grad.astype(jnp.bfloat16),
    )


def local(features, in_proj, short_taps, long_filter, out_grad):
    channels = out_grad.shape[0]
    tok_rows = features.shape[1]
    whole_proj = lax.all_gather(in_proj, ("narrow", "wide"), axis=0, tiled=True)
    projected = jnp.dot(whole_proj, features, preferred_element_type=jnp.float32)
    before = from_behind(projected[:, tok_rows - 2 :], ("narrow", "wide"), 1)
    extended = jnp.concatenate([before, projected], axis=1)
    tap_zero = short_taps[0][:, None]
    tap_one = short_taps[1][:, None]
    tap_two = short_taps[2][:, None]
    featured = (
        tap_zero * extended[:, 2:]
        + tap_one * extended[:, 1 : tok_rows + 1]
        + tap_two * extended[:, :tok_rows]
    )
    query_part = featured[:channels]
    key_part = featured[channels : 2 * channels]
    value_part = featured[2 * channels :]
    gated = (key_part * value_part).astype(jnp.bfloat16)
    conv_grad = (out_grad.astype(jnp.float32) * query_part).astype(jnp.bfloat16)
    gated_ch, filter_ch, cot_ch = (
        lax.all_to_all(gated, ("narrow", "wide"), split_axis=0, concat_axis=1, tiled=True),
        lax.all_to_all(long_filter, ("narrow", "wide"), split_axis=0, concat_axis=1, tiled=True),
        lax.all_to_all(conv_grad, ("narrow", "wide"), split_axis=0, concat_axis=1, tiled=True),
    )
    conv_ch, ggrad_ch, fgrad_ch = convolve_channels(gated_ch, filter_ch, cot_ch)
    convolved, gate_grad, filter_grad = (
        lax.all_to_all(conv_ch, ("narrow", "wide"), split_axis=1, concat_axis=0, tiled=True),
        lax.all_to_all(ggrad_ch, ("narrow", "wide"), split_axis=1, concat_axis=0, tiled=True),
        lax.all_to_all(fgrad_ch, ("narrow", "wide"), split_axis=1, concat_axis=0, tiled=True),
    )
    conv_wide = convolved.astype(jnp.float32)
    mixed_out = (query_part * conv_wide).astype(jnp.bfloat16)
    gate_wide = gate_grad.astype(jnp.float32)
    feat_deriv = jnp.concatenate(
        [out_grad.astype(jnp.float32) * conv_wide, gate_wide * value_part, gate_wide * key_part],
        axis=0,
    )
    after = from_behind(feat_deriv[:, :2], ("narrow", "wide"), -1)
    deriv_ext = jnp.concatenate([feat_deriv, after], axis=1)
    proj_deriv = (
        tap_zero * feat_deriv
        + tap_one * deriv_ext[:, 1 : tok_rows + 1]
        + tap_two * deriv_ext[:, 2:]
    ).astype(jnp.bfloat16)
    taps_part = jnp.stack(
        [
            jnp.sum(feat_deriv * extended[:, 2 - offset : 2 - offset + tok_rows], axis=1)
            for offset in range(3)
        ],
        axis=0,
    )
    taps_grad = lax.psum(taps_part, ("narrow", "wide"))
    proj_grad = lax.psum_scatter(
        lax.dot_general(
            proj_deriv, features, (((1,), (1,)), ((), ())), preferred_element_type=jnp.float32
        ),
        ("narrow", "wide"),
        scatter_dimension=0,
        tiled=True,
    )
    feat_grad = lax.dot_general(
        whole_proj, proj_deriv, (((0,), (0,)), ((), ())), preferred_element_type=jnp.float32
    ).astype(jnp.bfloat16)
    return (mixed_out, feat_grad, filter_grad, taps_grad, proj_grad)


def solution(mesh):
    placed = (
        P(None, ("narrow", "wide")),
        P(("narrow", "wide"), None),
        P(),
        P(None, ("narrow", "wide")),
        P(None, ("narrow", "wide")),
    )
    return jax.shard_map(
        local,
        mesh=mesh,
        in_specs=placed,
        out_specs=(
            P(None, ("narrow", "wide")),
            P(None, ("narrow", "wide")),
            P(None, ("narrow", "wide")),
            P(),
            P(("narrow", "wide"), None),
        ),
        check_vma=False,
    )
```

profile of v0, /device:TPU:0, one launch (start us, length us, event | category | flops | bytes accessed | tf_op | source)
XLA Modules:
  0.0 1119.1 jit_solution(16845854060698830892)
XLA Ops:
  7.9 11.1 all-to-all-start
  20.7 7.7 all-to-all-done
  32.7 292.6 %all-gather.3.cloned.1.call-done = bf16[128,6,4096]{2,1,0:T(8,128)(2,1)} async-done(((bf16[1,6,4096]{2,1,0:T(8,128)(2,1)}), bf16[128,6,4096]{2,1,0:T(8,128)(2,1)}) %all-gather.3.cloned.1.call-update) | async-done | bytes 6291472 | tf_op jit(solution)/shard_map/all_gather | solution.py:92
  325.3 10.2 reshape.98
  335.5 4.6 fusion.308
  345.2 7.3 collective-permute-done
  353.8 12.8 %all-to-all-start.3 = ((bf16[128,2,128]{2,1,0:T(2,128)(2,1)}), bf16[128,2,128]{2,1,0:T(2,128)(2,1)S(1)}, u32[]{:S(2)}, u32[]{:S(2)}) async-start(bf16[128,2,128]{2,1,0:T(2,128)(2,1)} %bitcast.17), calls=%async_computation.3 | async-start | bytes 131072 | tf_op jit(solution)/shard_map/all_to_all | solution.py:112
  369.7 6.2 all-to-all-done.3
  375.9 5.0 all-to-all-start.1
  381.8 8.1 all-to-all-done.1
  412.2 5.0 all-to-all-start.4
  429.0 9.9 all-to-all-start.2
  438.9 9.2 all-to-all-done.2
  450.2 11.6 %collective-permute-done.1 = f32[768,2]{1,0:T(8,128)S(1)} collective-permute-done((f32[768,2]{1,0:T(8,128)S(1)}, f32[768,2]{1,0:T(8,128)S(1)}, u32[]{:S(2)}, u32[]{:S(2)}) %collective-permute-start.1) | collective-permute-done | bytes 6176 | tf_op jit(solution)/shard_map/ppermute | solution.py:14
  463.1 6.4 fusion.309
  469.4 385.6 %fusion = f32[8,4096]{1,0:T(8,128)S(1)} fusion(f32[768,4096]{1,0:T(8,128)} %fusion.309), kind=kCustom, calls=%all-reduce-scatter | all-reduce-scatter fusion | flops 4194305 | bytes 12713984
  870.2 12.4 %collective-permute-start.24 = (f32[8,4096]{1,0:T(8,128)S(1)}, f32[8,4096]{1,0:T(8,128)S(1)}, u32[]{:S(2)}, u32[]{:S(2)}) collective-permute-start(f32[8,4096]{1,0:T(8,128)S(1)} %fusion), channel_id=1, source_target_pairs={{0,23},{1,24},{2,25},{3,26},{4,27},{5,28},{6,29},{7,30},{8,31},{9,... | collective-permute-start | bytes 393224
  882.7 3.8 collective-permute-start.23
  886.4 4.0 collective-permute-start.22
  894.7 10.9 collective-permute-start.19
  911.2 4.5 collective-permute-start.16
  915.8 8.2 collective-permute-start.15
  929.8 5.8 collective-permute-start.11
  938.6 8.2 collective-permute-start.8
  949.7 5.4 all-to-all-start.5
  955.1 9.2 all-to-all-done.5
  964.4 3.8 collective-permute-start.6
  968.2 4.4 collective-permute-start.5
  975.5 3.6 collective-permute-start.3
  982.8 3.8 fusion.1
  987.9 64.5 %psum.7 = f32[3,768]{1,0:T(4,128)} all-reduce(f32[3,768]{1,0:T(4,128)S(1)} %pad_maximum_fusion.3), channel_id=1, replica_groups=mesh['narrow'=16,'wide'=8] {'narrow','wide'}, use_global_device_ids=true, to_apply=%region_3.4 | all-reduce | flops 2304 | bytes 18432 | tf_op jit(solution)/shard_map/psum | solution.py:141
  1052.5 57.0 %concatenate.12 = f32[262,4096]{1,0:T(8,128)} concatenate(f32[6,4096]{1,0:T(8,128)S(1)} %collective-permute-done.33, f32[8,4096]{1,0:T(8,128)S(1)} %collective-permute-done.32, f32[8,4096]{1,0:T(8,128)S(1)} %copy-done.6, f32[8,4096]{1,0:T(8,128)S(1)} %copy-done.8, f32[8,4096]{1,0:T(8,128)S(1)} %copy-done.10, f32[8,4096]{1,0:T(8,128)S(1)} %copy-done.12, f32[8,4096]{1,0:T(8,128)S(1)} %copy-done.14, ...), dimensions={0} | concatenate | bytes 8585216
  (197 shorter events, 100.5 us)
Async XLA Ops:
  7.2 318.1 %all-gather.3.cloned.1.call-start = ((), (), s32[]{:S(2)}) async-start(), calls=%async_computation.6 | async-start | bytes 8454144 | tf_op jit(solution)/shard_map/all_gather | solution.py:92
  7.9 20.4 %all-to-all-start = ((bf16[128,2,128]{2,1,0:T(2,128)(2,1)}), bf16[128,2,128]{2,1,0:T(2,128)(2,1)S(1)}, u32[]{:S(2)}, u32[]{:S(2)}) async-start(bf16[128,2,128]{2,1,0:T(2,128)(2,1)} %bitcast.152), calls=%async_computation | async-start | bytes 131072 | tf_op jit(solution)/shard_map/all_to_all | solution.py:111
  353.8 22.0 %all-to-all-start.3 = ((bf16[128,2,128]{2,1,0:T(2,128)(2,1)}), bf16[128,2,128]{2,1,0:T(2,128)(2,1)S(1)}, u32[]{:S(2)}, u32[]{:S(2)}) async-start(bf16[128,2,128]{2,1,0:T(2,128)(2,1)} %bitcast.17), calls=%async_computation.3 | async-start | bytes 131072 | tf_op jit(solution)/shard_map/all_to_all | solution.py:112
  375.9 14.0 %all-to-all-start.1 = ((bf16[128,2,128]{2,1,0:T(2,128)(2,1)}), bf16[128,2,128]{2,1,0:T(2,128)(2,1)S(1)}, u32[]{:S(2)}, u32[]{:S(2)}) async-start(bf16[128,2,128]{2,1,0:T(2,128)(2,1)} %bitcast.9), calls=%async_computation.1 | async-start | bytes 131072 | tf_op jit(solution)/shard_map/all_to_all | solution.py:110
  412.2 16.8 %all-to-all-start.4 = ((bf16[2,128,128]{2,0,1:T(2,128)(2,1)}), bf16[2,128,128]{2,0,1:T(2,128)(2,1)S(1)}, u32[]{:S(2)}, u32[]{:S(2)}) async-start(bf16[2,128,128]{2,0,1:T(2,128)(2,1)} %copy.106), calls=%async_computation.4 | async-start | bytes 131072 | tf_op jit(solution)/shard_map/all_to_all | solution.py:117
  429.0 19.1 %all-to-all-start.2 = ((bf16[2,128,128]{2,0,1:T(2,128)(2,1)}), bf16[2,128,128]{2,0,1:T(2,128)(2,1)S(1)}, u32[]{:S(2)}, u32[]{:S(2)}) async-start(bf16[2,128,128]{2,0,1:T(2,128)(2,1)} %copy.94), calls=%async_computation.2 | async-start | bytes 131072 | tf_op jit(solution)/shard_map/all_to_all | solution.py:116
  863.4 19.2 %collective-permute-start.28 = (f32[8,4096]{1,0:T(8,128)S(1)}, f32[8,4096]{1,0:T(8,128)S(1)}, u32[]{:S(2)}, u32[]{:S(2)}) collective-permute-start(f32[8,4096]{1,0:T(8,128)S(1)} %fusion), channel_id=1, source_target_pairs={{0,27},{1,28},{2,29},{3,30},{4,31},{5,32},{6,33},{7,34},{8,35},{9,... | collective-permute-start | bytes 393224
  864.7 21.7 %collective-permute-start.27 = (f32[8,4096]{1,0:T(8,128)S(1)}, f32[8,4096]{1,0:T(8,128)S(1)}, u32[]{:S(2)}, u32[]{:S(2)}) collective-permute-start(f32[8,4096]{1,0:T(8,128)S(1)} %fusion), channel_id=1, source_target_pairs={{0,26},{1,27},{2,28},{3,29},{4,30},{5,31},{6,32},{7,33},{8,34},{9,... | collective-permute-start | bytes 393224
  867.6 24.4 %collective-permute-start.26 = (f32[8,4096]{1,0:T(8,128)S(1)}, f32[8,4096]{1,0:T(8,128)S(1)}, u32[]{:S(2)}, u32[]{:S(2)}) collective-permute-start(f32[8,4096]{1,0:T(8,128)S(1)} %fusion), channel_id=1, source_target_pairs={{0,25},{1,26},{2,27},{3,28},{4,29},{5,30},{6,31},{7,32},{8,33},{9,... | collective-permute-start | bytes 393224
  868.9 24.4 %collective-permute-start.25 = (f32[8,4096]{1,0:T(8,128)S(1)}, f32[8,4096]{1,0:T(8,128)S(1)}, u32[]{:S(2)}, u32[]{:S(2)}) collective-permute-start(f32[8,4096]{1,0:T(8,128)S(1)} %fusion), channel_id=1, source_target_pairs={{0,24},{1,25},{2,26},{3,27},{4,28},{5,29},{6,30},{7,31},{8,32},{9,... | collective-permute-start | bytes 393224
  870.2 24.4 %collective-permute-start.24 = (f32[8,4096]{1,0:T(8,128)S(1)}, f32[8,4096]{1,0:T(8,128)S(1)}, u32[]{:S(2)}, u32[]{:S(2)}) collective-permute-start(f32[8,4096]{1,0:T(8,128)S(1)} %fusion), channel_id=1, source_target_pairs={{0,23},{1,24},{2,25},{3,26},{4,27},{5,28},{6,29},{7,30},{8,31},{9,... | collective-permute-start | bytes 393224
  882.7 22.9 %collective-permute-start.23 = (f32[8,4096]{1,0:T(8,128)S(1)}, f32[8,4096]{1,0:T(8,128)S(1)}, u32[]{:S(2)}, u32[]{:S(2)}) collective-permute-start(f32[8,4096]{1,0:T(8,128)S(1)} %fusion), channel_id=1, source_target_pairs={{0,22},{1,23},{2,24},{3,25},{4,26},{5,27},{6,28},{7,29},{8,30},{9,... | collective-permute-start | bytes 393224
  886.4 21.1 %collective-permute-start.22 = (f32[8,4096]{1,0:T(8,128)S(1)}, f32[8,4096]{1,0:T(8,128)S(1)}, u32[]{:S(2)}, u32[]{:S(2)}) collective-permute-start(f32[8,4096]{1,0:T(8,128)S(1)} %fusion), channel_id=1, source_target_pairs={{0,21},{1,22},{2,23},{3,24},{4,25},{5,26},{6,27},{7,28},{8,29},{9,... | collective-permute-start | bytes 393224
  892.0 19.2 %collective-permute-start.21 = (f32[8,4096]{1,0:T(8,128)S(1)}, f32[8,4096]{1,0:T(8,128)S(1)}, u32[]{:S(2)}, u32[]{:S(2)}) collective-permute-start(f32[8,4096]{1,0:T(8,128)S(1)} %fusion), channel_id=1, source_target_pairs={{0,20},{1,21},{2,22},{3,23},{4,24},{5,25},{6,26},{7,27},{8,28},{9,... | collective-permute-start | bytes 393224
  893.4 22.4 %collective-permute-start.20 = (f32[8,4096]{1,0:T(8,128)S(1)}, f32[8,4096]{1,0:T(8,128)S(1)}, u32[]{:S(2)}, u32[]{:S(2)}) collective-permute-start(f32[8,4096]{1,0:T(8,128)S(1)} %fusion), channel_id=1, source_target_pairs={{0,19},{1,20},{2,21},{3,22},{4,23},{5,24},{6,25},{7,26},{8,27},{9,... | collective-permute-start | bytes 393224
  894.7 29.3 %collective-permute-start.19 = (f32[8,4096]{1,0:T(8,128)S(1)}, f32[8,4096]{1,0:T(8,128)S(1)}, u32[]{:S(2)}, u32[]{:S(2)}) collective-permute-start(f32[8,4096]{1,0:T(8,128)S(1)} %fusion), channel_id=1, source_target_pairs={{0,18},{1,19},{2,20},{3,21},{4,22},{5,23},{6,24},{7,25},{8,26},{9,... | collective-permute-start | bytes 393224
  905.6 20.4 %collective-permute-start.18 = (f32[8,4096]{1,0:T(8,128)S(1)}, f32[8,4096]{1,0:T(8,128)S(1)}, u32[]{:S(2)}, u32[]{:S(2)}) collective-permute-start(f32[8,4096]{1,0:T(8,128)S(1)} %fusion), channel_id=1, source_target_pairs={{0,17},{1,18},{2,19},{3,20},{4,21},{5,22},{6,23},{7,24},{8,25},{9,... | collective-permute-start | bytes 393224
  907.6 19.7 %collective-permute-start.17 = (f32[8,4096]{1,0:T(8,128)S(1)}, f32[8,4096]{1,0:T(8,128)S(1)}, u32[]{:S(2)}, u32[]{:S(2)}) collective-permute-start(f32[8,4096]{1,0:T(8,128)S(1)} %fusion), channel_id=1, source_target_pairs={{0,16},{1,17},{2,18},{3,19},{4,20},{5,21},{6,22},{7,23},{8,24},{9,... | collective-permute-start | bytes 393224
  911.2 18.5 %collective-permute-start.16 = (f32[8,4096]{1,0:T(8,128)S(1)}, f32[8,4096]{1,0:T(8,128)S(1)}, u32[]{:S(2)}, u32[]{:S(2)}) collective-permute-start(f32[8,4096]{1,0:T(8,128)S(1)} %fusion), channel_id=1, source_target_pairs={{0,15},{1,16},{2,17},{3,18},{4,19},{5,20},{6,21},{7,22},{8,23},{9,... | collective-permute-start | bytes 393224
  915.8 19.8 %collective-permute-start.15 = (f32[8,4096]{1,0:T(8,128)S(1)}, f32[8,4096]{1,0:T(8,128)S(1)}, u32[]{:S(2)}, u32[]{:S(2)}) collective-permute-start(f32[8,4096]{1,0:T(8,128)S(1)} %fusion), channel_id=1, source_target_pairs={{0,14},{1,15},{2,16},{3,17},{4,18},{5,19},{6,20},{7,21},{8,22},{9,... | collective-permute-start | bytes 393224
  927.9 18.9 %collective-permute-start.12 = (f32[8,4096]{1,0:T(8,128)S(1)}, f32[8,4096]{1,0:T(8,128)S(1)}, u32[]{:S(2)}, u32[]{:S(2)}) collective-permute-start(f32[8,4096]{1,0:T(8,128)S(1)} %fusion), channel_id=1, source_target_pairs={{0,11},{1,12},{2,13},{3,14},{4,15},{5,16},{6,17},{7,18},{8,19},{9,... | collective-permute-start | bytes 393224
  929.8 34.6 %collective-permute-start.11 = (f32[8,4096]{1,0:T(8,128)S(1)}, f32[8,4096]{1,0:T(8,128)S(1)}, u32[]{:S(2)}, u32[]{:S(2)}) collective-permute-start(f32[8,4096]{1,0:T(8,128)S(1)} %fusion), channel_id=1, source_target_pairs={{0,10},{1,11},{2,12},{3,13},{4,14},{5,15},{6,16},{7,17},{8,18},{9,... | collective-permute-start | bytes 393224
  935.6 32.5 %collective-permute-start.10 = (f32[8,4096]{1,0:T(8,128)S(1)}, f32[8,4096]{1,0:T(8,128)S(1)}, u32[]{:S(2)}, u32[]{:S(2)}) collective-permute-start(f32[8,4096]{1,0:T(8,128)S(1)} %fusion), channel_id=1, source_target_pairs={{0,9},{1,10},{2,11},{3,12},{4,13},{5,14},{6,15},{7,16},{8,17},{9,1... | collective-permute-start | bytes 393224
  937.3 35.3 %collective-permute-start.9 = (f32[8,4096]{1,0:T(8,128)S(1)}, f32[8,4096]{1,0:T(8,128)S(1)}, u32[]{:S(2)}, u32[]{:S(2)}) collective-permute-start(f32[8,4096]{1,0:T(8,128)S(1)} %fusion), channel_id=1, source_target_pairs={{0,8},{1,9},{2,10},{3,11},{4,12},{5,13},{6,14},{7,15},{8,16},{9,17... | collective-permute-start | bytes 393224
  938.6 36.9 %collective-permute-start.8 = (f32[8,4096]{1,0:T(8,128)S(1)}, f32[8,4096]{1,0:T(8,128)S(1)}, u32[]{:S(2)}, u32[]{:S(2)}) collective-permute-start(f32[8,4096]{1,0:T(8,128)S(1)} %fusion), channel_id=1, source_target_pairs={{0,7},{1,8},{2,9},{3,10},{4,11},{5,12},{6,13},{7,14},{8,15},{9,16}... | collective-permute-start | bytes 393224
  947.0 32.1 %collective-permute-start.7 = (f32[8,4096]{1,0:T(8,128)S(1)}, f32[8,4096]{1,0:T(8,128)S(1)}, u32[]{:S(2)}, u32[]{:S(2)}) collective-permute-start(f32[8,4096]{1,0:T(8,128)S(1)} %fusion), channel_id=1, source_target_pairs={{0,6},{1,7},{2,8},{3,9},{4,10},{5,11},{6,12},{7,13},{8,14},{9,15},... | collective-permute-start | bytes 393224
  949.7 14.6 %all-to-all-start.5 = ((bf16[2,128,128]{2,0,1:T(2,128)(2,1)}), bf16[2,128,128]{2,0,1:T(2,128)(2,1)S(1)}, u32[]{:S(2)}, u32[]{:S(2)}) async-start(bf16[2,128,128]{2,0,1:T(2,128)(2,1)} %copy.113), calls=%async_computation.5 | async-start | bytes 131072 | tf_op jit(solution)/shard_map/all_to_all | solution.py:118
  964.4 88.1 %collective-permute-start.6 = (f32[8,4096]{1,0:T(8,128)S(1)}, f32[8,4096]{1,0:T(8,128)}, u32[]{:S(2)}, u32[]{:S(2)}) collective-permute-start(f32[8,4096]{1,0:T(8,128)S(1)} %fusion), channel_id=1, source_target_pairs={{0,5},{1,6},{2,7},{3,8},{4,9},{5,10},{6,11},{7,12},{8,13},{9,14},{... | collective-permute-start | bytes 393224
  968.2 84.3 %collective-permute-start.5 = (f32[8,4096]{1,0:T(8,128)S(1)}, f32[8,4096]{1,0:T(8,128)}, u32[]{:S(2)}, u32[]{:S(2)}) collective-permute-start(f32[8,4096]{1,0:T(8,128)S(1)} %fusion), channel_id=1, source_target_pairs={{0,4},{1,5},{2,6},{3,7},{4,8},{5,9},{6,10},{7,11},{8,12},{9,13},{1... | collective-permute-start | bytes 393224
  972.6 79.9 %collective-permute-start.4 = (f32[8,4096]{1,0:T(8,128)S(1)}, f32[8,4096]{1,0:T(8,128)}, u32[]{:S(2)}, u32[]{:S(2)}) collective-permute-start(f32[8,4096]{1,0:T(8,128)S(1)} %fusion), channel_id=1, source_target_pairs={{0,3},{1,4},{2,5},{3,6},{4,7},{5,8},{6,9},{7,10},{8,11},{9,12},{10... | collective-permute-start | bytes 393224
  975.5 77.0 %collective-permute-start.3 = (f32[8,4096]{1,0:T(8,128)S(1)}, f32[8,4096]{1,0:T(8,128)}, u32[]{:S(2)}, u32[]{:S(2)}) collective-permute-start(f32[8,4096]{1,0:T(8,128)S(1)} %fusion), channel_id=1, source_target_pairs={{0,2},{1,3},{2,4},{3,5},{4,6},{5,7},{6,8},{7,9},{8,10},{9,11},{10,... | collective-permute-start | bytes 393224
  979.8 72.7 %collective-permute-start.2 = (f32[8,4096]{1,0:T(8,128)S(1)}, f32[8,4096]{1,0:T(8,128)}, u32[]{:S(2)}, u32[]{:S(2)}) collective-permute-start(f32[8,4096]{1,0:T(8,128)S(1)} %fusion), channel_id=1, source_target_pairs={{0,1},{1,2},{2,3},{3,4},{4,5},{5,6},{6,7},{7,8},{8,9},{9,10},{10,1... | collective-permute-start | bytes 393224
  (44 other events, 2176.8 us)
Sparse Core Ops, SparseCore 0:
  9.7 315.5 all-gather.2
where the time goes:
time: 1130 us; the launch traced here: 1120 us
  blocking collectives  450 us (40%)
  waiting for transfers between devices  353 us (31%)
  starting transfers between devices  156 us (14%)
  local copies, waits for them, and re-layouts  75.8 us (7%)
  matrix products  64.6 us (6%)
  between operations  15.8 us (1%)
    unnamed x1, blocking collectives  386 us
    all_gather x1, waiting for transfers between devices, local(): whole_proj = lax.all_gather(in_proj, ('narrow', 'wide'), axis=0, tiled=True)  293 us
    unnamed x32, starting transfers between devices  103 us
    unnamed x76, local copies, waits for them, and re-layouts  72.3 us
    psum x1, blocking collectives, local(): taps_grad = lax.psum(taps_part, ('narrow', 'wide'))  64.5 us
  transfers between devices with their start and end apart: 41, of which 8 were waited for; matrix products, arithmetic and copies ran while one was open for 3% of the time, Pallas kernels for 0%

commit v1 on v0

v1 whole, which is shorter than its diff:
```python
import math

import jax
import jax.numpy as jnp
from jax import lax
from jax.experimental import pallas as pl
from jax.experimental.pallas import tpu as pltpu
from jax.sharding import PartitionSpec as P

MESH = pl.DeviceIdType.MESH
BF = jnp.bfloat16
F32 = jnp.float32
ORDERS = (("x", "y", "z"), ("y", "z", "x"), ("z", "x", "y"))
AXES = ("narrow", "wide")


def place(pos):
    y = pos["y"]
    return (pos["z"] * 4 + lax.rem(y, 2) * 2 + pos["c"], (y // 2) * 4 + pos["x"])


def position():
    n = lax.axis_index("narrow")
    w = lax.axis_index("wide")
    pos = {
        "x": lax.rem(w, 4),
        "y": (w // 4) * 2 + lax.rem(n // 2, 2),
        "z": n // 4,
        "c": lax.rem(n, 2),
    }
    return n, w, pos


def shifted(pos, axis, by):
    other = dict(pos)
    other[axis] = lax.rem(pos[axis] + by + 4, 4)
    return place(other)


def other_core(pos):
    other = dict(pos)
    other["c"] = 1 - pos["c"]
    return place(other)


def shard_id(s):
    return (s // 8, lax.rem(s, 8))


def remote(src, dst, send, recv, device):
    return pltpu.make_async_remote_copy(
        src_ref=src, dst_ref=dst, send_sem=send, recv_sem=recv, device_id=device, device_id_type=MESH
    )


def greet(devices):
    barrier = pltpu.get_barrier_semaphore()
    for device in devices:
        pl.semaphore_signal(barrier, inc=1, device_id=device, device_id_type=MESH)
    pl.semaphore_wait(barrier, len(devices))


def piece_index(cls, z, yh, yl, x):
    at = {"x": x, "y": yh * 2 + yl, "z": z}
    d0, d1, d2 = ORDERS[cls]
    return (at[d2], at[d1], at[d0])


def one_hot(rows, cols, test):
    r = lax.broadcasted_iota(jnp.int32, (rows, cols), 0)
    c = lax.broadcasted_iota(jnp.int32, (rows, cols), 1)
    return jnp.where(test(r, c), 1.0, 0.0).astype(BF)


def gather_kernel(
    proj_ref, feat_ref, out_ref, halo_ref, g_ref, fo_ref,
    stage, land, blk, rows, hland, fh,
    s0, r0, ss, rs, ds, dr, hs, hr, fs, fr,
):
    n, w, pos = position()
    c = pos["c"]
    s = n * 8 + w
    right_shard = shard_id(lax.rem(s + 1, 128))
    left_shard = shard_id(lax.rem(s + 127, 128))
    wide_peers = [(n, lax.rem(w + i, 8)) for i in range(1, 8)]
    core = other_core(pos)
    for q in range(8):
        stage[q, 0:6, :] = proj_ref[:, q * 512 : (q + 1) * 512].astype(F32)
        stage[q, 6:8, :] = jnp.zeros((2, 512), F32)
    greet(
        wide_peers
        + [shifted(pos, a, d) for a in "yz" for d in (1, -1)]
        + [core, right_shard, left_shard]
    )
    first = []
    for i in range(1, 8):
        q = lax.rem(w + i, 8)
        cp = remote(stage.at[q], land.at[w], s0.at[i], r0.at[i], (n, q))
        cp.start()
        first.append(cp)
    fcp = remote(feat_ref, fo_ref, fs, fr, core)
    land[w] = stage[w]
    for cp in first:
        cp.wait_recv()
    for q in range(8):
        blk[q * 6 : (q + 1) * 6, :] = land[q, 0:6, :]

    index = [[pos[a] for a in reversed(order)] for order in ORDERS]
    for cls in range(3):
        i2, i1, i0 = index[cls]
        g_ref[cls, c, i2, i1, i0] = blk[cls * 16 : (cls + 1) * 16, :].astype(BF)

    def unit(cls, phase, j):
        i2, i1, _ = index[cls]
        if phase == 0:
            return g_ref.at[cls, c, i2, i1, j]
        if phase == 1:
            return g_ref.at[cls, c, i2, j]
        return g_ref.at[cls, c, j]

    def half(ref, phase, k):
        if phase == 0:
            return ref.at[:, pl.ds(k * 256, 256)]
        return ref.at[pl.ds(k * 2, 2)]

    started = [first[k] for k in range(7)]
    d2d = []

    def cross(cls, j, k):
        ref = g_ref.at[cls, c, j]
        cp = remote(ref, ref, ds.at[cls, k], dr.at[cls, k], core)
        cp.start()
        d2d.append(cp)

    for phase in range(3):
        legs = []
        for cls in range(3):
            axis = ORDERS[cls][phase]
            i = pos[axis]
            right, left = shifted(pos, axis, 1), shifted(pos, axis, -1)
            mine = unit(cls, phase, i)
            a = remote(mine, mine, ss.at[cls, phase, 0], rs.at[cls, phase, 0], right)
            b = remote(mine, mine, ss.at[cls, phase, 1], rs.at[cls, phase, 1], left)
            a.start()
            b.start()
            legs.append((a, b, right, left, i))
            if phase == 2:
                cross(cls, i, 0)
        if phase == 0:
            sel = one_hot(
                16, 128, lambda r, l: ((r < 2) & (l == r + 126)) | ((r >= 2) & (r < 4) & (l == r - 2))
            )
            rows[...] = lax.dot_general(
                sel, feat_ref[...], (((1,), (1,)), ((), ())), preferred_element_type=F32
            ).astype(BF)
            ha = remote(rows, hland.at[0], hs.at[0], hr.at[0], right_shard)
            hb = remote(rows, hland.at[1], hs.at[1], hr.at[1], left_shard)
            ha.start()
            hb.start()
            fcp.start()
            fh[:, 0:128] = feat_ref[...]
        if phase == 2:
            ha.wait_recv()
            hb.wait_recv()
            row = lax.broadcasted_iota(jnp.int32, (16, 4096), 0)
            both = jnp.where(row < 2, hland[0].astype(F32), hland[1].astype(F32)).astype(BF)
            lo = jnp.where(s > 0, 0, 2)
            hi = jnp.where(s < 127, 4, 2)
            spread = one_hot(16, 128, lambda r, l: (r == l) & (r >= lo) & (r < hi))
            fh[:, 128:256] = lax.dot_general(
                both, spread, (((0,), (0,)), ((), ())), preferred_element_type=F32
            ).astype(BF)
        second = []
        for cls in range(3):
            a, b, right, left, i = legs[cls]
            started += [a, b]
            a.wait_recv()
            got = unit(cls, phase, lax.rem(i + 3, 4))
            e = half(got, phase, 0)
            e = remote(e, e, ss.at[cls, phase, 2], rs.at[cls, phase, 2], right)
            e.start()
            b.wait_recv()
            got = unit(cls, phase, lax.rem(i + 1, 4))
            f = half(got, phase, 1)
            f = remote(f, f, ss.at[cls, phase, 3], rs.at[cls, phase, 3], left)
            f.start()
            second.append((e, f))
            if phase == 2:
                cross(cls, lax.rem(i + 3, 4), 1)
                cross(cls, lax.rem(i + 1, 4), 2)
        for cls in range(3):
            e, f = second[cls]
            started += [e, f]
            e.wait_recv()
            f.wait_recv()
            if phase == 2:
                cross(cls, lax.rem(legs[cls][4] + 2, 4), 3)
    for cp in d2d:
        cp.wait_recv()

    for cls in range(3):
        acc = None
        for yh in range(2):
            for x in range(4):
                lhs = wide_block(g_ref, cls, yh, x)
                q = yh * 4 + x
                term = jnp.dot(lhs, fh[q * 512 : (q + 1) * 512, :], preferred_element_type=F32)
                acc = term if acc is None else acc + term
        for m in range(16):
            out_ref[m * 48 + cls * 16 : m * 48 + cls * 16 + 16, :] = acc[m * 16 : (m + 1) * 16, 0:128]
            halo_ref[m * 48 + cls * 16 : m * 48 + cls * 16 + 16, :] = acc[m * 16 : (m + 1) * 16, 128:256]

    fcp.wait_recv()
    for cp in started + d2d + [ha, hb, fcp]:
        cp.wait_send()


def wide_block(g_ref, cls, yh, x):
    parts = []
    for z in range(4):
        for yl in range(2):
            for core in range(2):
                i2, i1, i0 = piece_index(cls, z, yh, yl, x)
                parts.append(g_ref[cls, core, i2, i1, i0])
    return jnp.concatenate(parts, axis=0)


VM = pl.BlockSpec(memory_space=pltpu.VMEM)


def gather_project(in_proj, features):
    sem = pltpu.SemaphoreType.DMA
    return pl.pallas_call(
        gather_kernel,
        out_shape=(
            jax.ShapeDtypeStruct((768, 128), F32),
            jax.ShapeDtypeStruct((768, 128), F32),
            jax.ShapeDtypeStruct((3, 2, 4, 4, 4, 16, 512), BF),
            jax.ShapeDtypeStruct((4096, 128), BF),
        ),
        in_specs=[VM, VM],
        out_specs=(VM, VM, VM, VM),
        scratch_shapes=[
            pltpu.VMEM((8, 8, 512), F32),
            pltpu.VMEM((8, 8, 512), F32),
            pltpu.VMEM((48, 512), F32),
            pltpu.VMEM((16, 4096), BF),
            pltpu.VMEM((2, 16, 4096), BF),
            pltpu.VMEM((4096, 256), BF),
            sem((8,)), sem((8,)),
            sem((3, 3, 4)), sem((3, 3, 4)),
            sem((3, 4)), sem((3, 4)),
            sem((2,)), sem((2,)),
            sem, sem,
        ],
        compiler_params=pltpu.CompilerParams(
            collective_id=1, has_side_effects=True, vmem_limit_bytes=48 * 1024 * 1024
        ),
        name="gather_project",
    )(in_proj, features)


def reduce_kernel(
    pd_ref, feat_ref, fo_ref, g_ref, taps_ref, grad_ref, fgrad_ref, tout_ref,
    pdo, pdc, p, ra3, rb3, rc3, rd3, ra2, rb2, rc2, rd2, ra1, rb1, rc1, rd1,
    blk, stage, land, tl,
    ps, pr, ss, rs, s0, r0, tsn, trc,
):
    n, w, pos = position()
    c = pos["c"]
    core = other_core(pos)
    wide_peers = [(n, lax.rem(w + i, 8)) for i in range(1, 8)]
    greet(
        wide_peers
        + [shifted(pos, a, d) for a in "yz" for d in (1, 2, 3)]
        + [core]
    )
    pcp = remote(pd_ref, pdo, ps, pr, core)
    pcp.start()

    sent = [pcp]

    def tap_send(k, peers, slot):
        cps = []
        for i, device in enumerate(peers):
            cp = remote(tl.at[k, slot], tl.at[k, slot], tsn.at[k, i], trc.at[k, i], device)
            cp.start()
            cps.append(cp)
        return cps

    def tap_sum(k, cps, count):
        for cp in cps:
            cp.wait_recv()
        sent.extend(cps)
        total = tl[k, 0]
        for i in range(1, count):
            total = total + tl[k, i]
        return total

    tl[0, c] = taps_ref[...]
    tcp = tap_send(0, [core], c)

    index = [[pos[a] for a in reversed(order)] for order in ORDERS]
    pcp.wait_recv()
    for cls in range(3):
        for z in range(4):
            for yl in range(2):
                at = pl.ds(pl.multiple_of((z * 4 + yl * 2 + c) * 48 + cls * 16, 16), 16)
                to = cls * 128 + z * 32 + yl * 16
                pdc[to : to + 16, 0:128] = pd_ref[at, :]
                pdc[to : to + 16, 128:256] = pdo[at, :]

    for yh in range(2):
        for x in range(4):
            cols = slice((yh * 4 + x) * 512, (yh * 4 + x + 1) * 512)
            rhs = jnp.concatenate([feat_ref[cols, :], fo_ref[cols, :]], axis=1)
            for cls in range(3):
                part = lax.dot_general(
                    pdc[cls * 128 : (cls + 1) * 128, :], rhs, (((1,), (1,)), ((), ())),
                    preferred_element_type=F32,
                ).astype(BF)
                for z in range(4):
                    for yl in range(2):
                        i2, i1, i0 = piece_index(cls, z, yh, yl, x)
                        k = z * 32 + yl * 16
                        p[cls, i2, i1, i0] = part[k : k + 16, :]

    def unit(cls, phase, j):
        i2, i1, _ = index[cls]
        if phase == 0:
            return p.at[cls, i2, i1, j]
        if phase == 1:
            return p.at[cls, i2, j]
        return p.at[cls, j]

    def half(ref, phase, k):
        if phase == 0:
            return ref.at[:, pl.ds(k * 256, 256)]
        return ref.at[pl.ds(k * 2, 2)]

    bufs = {2: (ra3, rb3, rc3, rd3), 1: (ra2, rb2, rc2, rd2), 0: (ra1, rb1, rc1, rd1)}

    def add(dst, src):
        dst[...] = (dst[...].astype(F32) + src[...].astype(F32)).astype(BF)

    def feat_part(qs):
        for q in qs:
            total = None
            for cls in range(3):
                lhs = jnp.concatenate(
                    [pd_ref[m * 48 + cls * 16 : m * 48 + cls * 16 + 16, :] for m in range(16)], axis=0
                )
                term = lax.dot_general(
                    lhs, wide_block(g_ref, cls, q // 4, q % 4), (((0,), (0,)), ((), ())),
                    preferred_element_type=F32,
                )
                total = term if total is None else total + term
            fgrad_ref[q * 512 : (q + 1) * 512, :] = total.T.astype(BF)

    for phase in (2, 1, 0):
        ra, rb, rc, rd = bufs[phase]
        legs = []
        for cls in range(3):
            axis = ORDERS[cls][phase]
            i = pos[axis]
            right, left = shifted(pos, axis, 1), shifted(pos, axis, -1)
            far = unit(cls, phase, lax.rem(i + 2, 4))
            up = unit(cls, phase, lax.rem(i + 1, 4))
            down = unit(cls, phase, lax.rem(i + 3, 4))

            def cp(k, src, dst, device):
                r = remote(src, dst, ss.at[cls, phase, k], rs.at[cls, phase, k], device)
                r.start()
                sent.append(r)
                return r

            a = cp(0, half(far, phase, 0), ra.at[cls], right)
            b = cp(1, half(far, phase, 1), rb.at[cls], left)
            d = cp(2, half(up, phase, 1), half(rc.at[cls], phase, 1), right)
            e = cp(3, half(down, phase, 0), half(rd.at[cls], phase, 0), left)
            legs.append((cp, a, b, d, e, up, down, right, left, i))
        if phase == 2:
            feat_part(range(4))
        if phase == 1:
            feat_part(range(6, 8))
        more = []
        for cls in range(3):
            cp, a, b, d, e, up, down, right, left, i = legs[cls]

            def cp(k, src, dst, device):
                r = remote(src, dst, ss.at[cls, phase, k], rs.at[cls, phase, k], device)
                r.start()
                sent.append(r)
                return r

            a.wait_recv()
            add(half(up, phase, 0), ra.at[cls])
            f = cp(4, half(up, phase, 0), half(rc.at[cls], phase, 0), right)
            b.wait_recv()
            add(half(down, phase, 1), rb.at[cls])
            g = cp(5, half(down, phase, 1), half(rd.at[cls], phase, 1), left)
            more.append((f, g))
        if phase == 2:
            t1 = tap_sum(0, tcp, 2)
            tl[1, pos["x"]] = t1
            tcp = tap_send(1, [shifted(pos, "x", d) for d in (1, 2, 3)], pos["x"])
            feat_part(range(4, 6))
        if phase == 1:
            t1 = tap_sum(1, tcp, 4)
            tl[2, pos["y"]] = t1
            tcp = tap_send(2, [shifted(pos, "y", d) for d in (1, 2, 3)], pos["y"])
        if phase == 0:
            t1 = tap_sum(2, tcp, 4)
            tl[3, pos["z"]] = t1
            tcp = tap_send(3, [shifted(pos, "z", d) for d in (1, 2, 3)], pos["z"])
        for cls in range(3):
            _, a, b, d, e, up, down, right, left, i = legs[cls]
            f, g = more[cls]
            for k in (d, e, f, g):
                k.wait_recv()
            mine = unit(cls, phase, i)
            total = mine[...].astype(F32) + rc[cls].astype(F32) + rd[cls].astype(F32)
            if phase == 0:
                blk[cls * 16 : (cls + 1) * 16, :] = total
            else:
                mine[...] = total.astype(BF)

    for q in range(8):
        stage[q, 0:6, :] = blk[q * 6 : (q + 1) * 6, :]
        stage[q, 6:8, :] = jnp.zeros((2, 512), F32)
    last = []
    for i in range(1, 8):
        q = lax.rem(w + i, 8)
        r = remote(stage.at[q], land.at[w], s0.at[i], r0.at[i], (n, q))
        r.start()
        last.append(r)
    land[w] = stage[w]
    tout_ref[...] = tap_sum(3, tcp, 4)
    for r in last:
        r.wait_recv()
    for q in range(8):
        grad_ref[:, q * 512 : (q + 1) * 512] = land[q, 0:6, :]
    for r in sent + last:
        r.wait_send()


def reduce_grads(pd, features, fo, g, taps):
    sem = pltpu.SemaphoreType.DMA
    return pl.pallas_call(
        reduce_kernel,
        out_shape=(
            jax.ShapeDtypeStruct((6, 4096), F32),
            jax.ShapeDtypeStruct((4096, 128), BF),
            jax.ShapeDtypeStruct((8, 768), F32),
        ),
        in_specs=[VM] * 5,
        out_specs=(VM,) * 3,
        scratch_shapes=[
            pltpu.VMEM((768, 128), BF),
            pltpu.VMEM((384, 256), BF),
            pltpu.VMEM((3, 4, 4, 4, 16, 512), BF),
            pltpu.VMEM((3, 2, 4, 16, 512), BF), pltpu.VMEM((3, 2, 4, 16, 512), BF),
            pltpu.VMEM((3, 4, 4, 16, 512), BF), pltpu.VMEM((3, 4, 4, 16, 512), BF),
            pltpu.VMEM((3, 2, 16, 512), BF), pltpu.VMEM((3, 2, 16, 512), BF),
            pltpu.VMEM((3, 4, 16, 512), BF), pltpu.VMEM((3, 4, 16, 512), BF),
            pltpu.VMEM((3, 16, 256), BF), pltpu.VMEM((3, 16, 256), BF),
            pltpu.VMEM((3, 16, 512), BF), pltpu.VMEM((3, 16, 512), BF),
            pltpu.VMEM((48, 512), F32),
            pltpu.VMEM((8, 8, 512), F32),
            pltpu.VMEM((8, 8, 512), F32),
            pltpu.VMEM((4, 4, 8, 768), F32),
            sem, sem,
            sem((3, 3, 6)), sem((3, 3, 6)),
            sem((8,)), sem((8,)),
            sem((4, 3)), sem((4, 3)),
        ],
        compiler_params=pltpu.CompilerParams(
            collective_id=2, has_side_effects=True, vmem_limit_bytes=56 * 1024 * 1024
        ),
        name="reduce_grads",
    )(pd, features, fo, g, taps)

def lanes(rows):
    return lax.broadcasted_iota(jnp.int32, (rows, 128), 1)


def toeplitz_conv(h_ref, ch, rhs):
    width = rhs.shape[1]
    groups = width // 128
    lane = lanes(128)
    row = lax.broadcasted_iota(jnp.int32, (128, 128), 0)
    upper = lane >= row

    def rolled(k):
        taps = jnp.broadcast_to(h_ref[ch, pl.ds(k, 1), :], (128, 128))
        return pltpu.roll(taps, 0, 1, stride=1, stride_axis=0)

    def step(i, carry):
        acc, top = carry
        m = 63 - i
        mid = rolled(2 * m)
        low = jnp.where(m > 0, rolled(jnp.maximum(2 * m - 1, 0)), 0.0)
        odd = jnp.where(upper, top, mid).astype(BF)
        even = jnp.where(upper, mid, low).astype(BF)
        lhs = jnp.concatenate([even, odd], axis=1)
        term = jnp.dot(lhs, rhs, preferred_element_type=F32)
        parts = []
        for g in range(groups):
            part = pltpu.roll(acc[:, g * 128 : (g + 1) * 128], 2, 1)
            parts.append(jnp.where(lane < 2, 0.0, part) + term[:, g * 128 : (g + 1) * 128])
        return jnp.concatenate(parts, axis=1) if groups > 1 else parts[0], low

    acc, _ = lax.fori_loop(0, 64, step, (jnp.zeros((128, width), F32), rolled(127)))
    return acc


def stacked(x):
    later = jnp.where(lanes(128) < 1, 0.0, pltpu.roll(x, 1, 1))
    return jnp.concatenate([x.astype(BF), later.astype(BF)], axis=0)


def middle_kernel(
    p_ref, halo_ref, taps_ref, og_ref, lf_ref,
    mixed_ref, fgout_ref, pd_ref, tp_ref,
    send, land, send2, land2, ogn, hf, gf, feat, featn,
    ss, rs, ss2, rs2, os, orr,
):
    n, w, pos = position()
    s = n * 8 + w
    barrier = pltpu.get_barrier_semaphore()

    @pl.loop(1, 128)
    def _(i):
        pl.semaphore_signal(
            barrier, inc=1, device_id=shard_id(lax.rem(s + i, 128)), device_id_type=MESH
        )

    lane = lanes(256)
    for part in range(3):
        at = slice(part * 256, (part + 1) * 256)
        p = p_ref[at, :]
        halo = halo_ref[at, :]
        t0, t1, t2 = taps_ref[at, 0:1], taps_ref[at, 1:2], taps_ref[at, 2:3]
        p1 = jnp.where(lane < 1, pltpu.roll(halo, 127, 1), pltpu.roll(p, 1, 1))
        p2 = jnp.where(lane < 2, halo, pltpu.roll(p, 2, 1))
        feat[part] = t0 * p + t1 * p1 + t2 * p2
        n1 = jnp.where(lane < 1, pltpu.roll(p, 1, 1), pltpu.roll(halo, 127, 1))
        featn[part] = t0 * pltpu.roll(halo, 126, 1) + t1 * n1 + t2 * pltpu.roll(p, 2, 1)
    og = og_ref[...].astype(F32)
    gated = (feat[1] * feat[2]).astype(BF).astype(F32)
    cot = (og * feat[0]).astype(BF).astype(F32)
    lf = lf_ref[...].astype(F32)
    for r in range(2):
        at = slice(r * 128, (r + 1) * 128)
        send[pl.ds(r, 128, stride=8), :] = gated[at]
        send[pl.ds(2 + r, 128, stride=8), :] = cot[at]
        send[pl.ds(4 + r, 128, stride=8), :] = lf[at]
        send[pl.ds(6 + r, 128, stride=8), :] = jnp.zeros((128, 128), F32)
    pl.semaphore_wait(barrier, 127)

    def tile(i):
        return pl.ds(pl.multiple_of(i * 8, 8), 8)

    def exchange(src, dst, a, b):
        @pl.loop(1, 128)
        def _(i):
            t = lax.rem(s + i, 128)
            remote(src.at[tile(t)], dst.at[tile(s)], a, b, shard_id(t)).start()

        dst[tile(s), :] = src[tile(s), :]
        whole = pl.ds(0, 127 * 8)
        return remote(src.at[whole], dst.at[whole], a, b, (n, w))

    go = exchange(send, land, ss, rs)
    ocp = remote(og_ref, ogn, os, orr, shard_id(lax.rem(s + 127, 128)))
    ocp.start()
    go.wait_recv()

    anti = one_hot(128, 128, lambda r, l: r + l == 127)
    dims = lambda a, b: (((a,), (b,)), ((), ()))
    row = lax.broadcasted_iota(jnp.int32, (128, 128), 0)
    lane1 = lanes(128)
    ahead = jnp.zeros((128, 128), F32)
    for ch in range(2):
        gate_in = land[pl.ds(ch, 128, stride=8), :]
        cot_in = land[pl.ds(2 + ch, 128, stride=8), :].astype(BF)
        hf[ch] = land[pl.ds(4 + ch, 128, stride=8), :]
        gf[ch] = gate_in
        xg = lax.dot_general(anti, gate_in.astype(BF), dims(1, 1), preferred_element_type=F32)
        xc = lax.dot_general(cot_in, anti, dims(0, 0), preferred_element_type=F32)
        xc2 = stacked(xc)
        out = toeplitz_conv(hf, ch, jnp.concatenate([stacked(xg), xc2], axis=1)).astype(BF)
        conv = lax.dot_general(out[:, 0:128], anti, dims(0, 0), preferred_element_type=F32)
        gg = lax.dot_general(anti, out[:, 128:256], dims(1, 1), preferred_element_type=F32)
        fg = toeplitz_conv(gf, ch, xc2).astype(BF)
        fg = lax.dot_general(anti, fg, dims(1, 1), preferred_element_type=F32)
        send2[pl.ds(ch, 128, stride=8), :] = conv
        send2[pl.ds(2 + ch, 128, stride=8), :] = gg
        send2[pl.ds(5 + ch, 128, stride=8), :] = fg
        for k, value in ((ch, conv), (2 + ch, gg)):
            nxt = jnp.where(row < 127, pltpu.roll(value, 127, 0), 0.0)
            moved = pltpu.roll(nxt, 2 * k, 1) if k else nxt
            ahead = jnp.where((lane1 >= 2 * k) & (lane1 < 2 * k + 2), moved, ahead)
    send2[pl.ds(4, 128, stride=8), :] = ahead
    send2[pl.ds(7, 128, stride=8), :] = jnp.zeros((128, 128), F32)

    back = exchange(send2, land2, ss2, rs2)
    ocp.wait_recv()
    back.wait_recv()

    def channels(r):
        return jnp.concatenate(
            [land2[pl.ds(r, 128, stride=8), :], land2[pl.ds(r + 1, 128, stride=8), :]], axis=0
        )

    conv, gg = channels(0), channels(2)
    fgout_ref[...] = channels(5).astype(BF)
    ahead = land2[pl.ds(4, 128, stride=8), :]
    convn = jnp.concatenate([ahead, pltpu.roll(ahead, 126, 1)], axis=0)
    ggn = jnp.concatenate([pltpu.roll(ahead, 124, 1), pltpu.roll(ahead, 122, 1)], axis=0)
    mixed_ref[...] = (feat[0] * conv).astype(BF)
    ogv = ogn[...].astype(F32)
    last = s == 127
    sums = []
    for part in range(3):
        at = slice(part * 256, (part + 1) * 256)
        if part == 0:
            fd, fdn = og * conv, ogv * convn
        else:
            fd, fdn = gg * feat[3 - part], ggn * featn[3 - part]
        fdn = jnp.where(last, 0.0, fdn)
        t0, t1, t2 = taps_ref[at, 0:1], taps_ref[at, 1:2], taps_ref[at, 2:3]
        f1 = jnp.where(lane < 127, pltpu.roll(fd, 127, 1), pltpu.roll(fdn, 127, 1))
        f2 = jnp.where(lane < 126, pltpu.roll(fd, 126, 1), pltpu.roll(fdn, 126, 1))
        pd_ref[at, :] = (t0 * fd + t1 * f1 + t2 * f2).astype(BF)
        p = p_ref[at, :]
        halo = halo_ref[at, :]
        p1 = jnp.where(lane < 1, pltpu.roll(halo, 127, 1), pltpu.roll(p, 1, 1))
        p2 = jnp.where(lane < 2, halo, pltpu.roll(p, 2, 1))
        total = jnp.zeros((256, 128), F32)
        for k, q in enumerate((p, p1, p2)):
            total = jnp.where(lane == k, jnp.sum(fd * q, axis=1, keepdims=True), total)
        sums.append(total)
    for part in range(3):
        tp_ref[:, part * 256 : (part + 1) * 256] = sums[part].T[0:8, :]
    go.wait_send()
    back.wait_send()
    ocp.wait_send()


def middle(projected, halo, taps, out_grad, long_filter):
    sem = pltpu.SemaphoreType.DMA
    return pl.pallas_call(
        middle_kernel,
        out_shape=(
            jax.ShapeDtypeStruct((256, 128), BF),
            jax.ShapeDtypeStruct((256, 128), BF),
            jax.ShapeDtypeStruct((768, 128), BF),
            jax.ShapeDtypeStruct((8, 768), F32),
        ),
        in_specs=[VM] * 5,
        out_specs=(VM,) * 4,
        scratch_shapes=[
            pltpu.VMEM((1024, 128), F32), pltpu.VMEM((1024, 128), F32),
            pltpu.VMEM((1024, 128), F32), pltpu.VMEM((1024, 128), F32),
            pltpu.VMEM((256, 128), BF),
            pltpu.VMEM((2, 128, 128), F32), pltpu.VMEM((2, 128, 128), F32),
            pltpu.VMEM((3, 256, 128), F32), pltpu.VMEM((3, 256, 128), F32),
            sem, sem, sem, sem, sem, sem,
        ],
        compiler_params=pltpu.CompilerParams(
            collective_id=3, has_side_effects=True, vmem_limit_bytes=32 * 1024 * 1024
        ),
        name="middle",
    )(projected, halo, taps, out_grad, long_filter)


def local(features, in_proj, short_taps, long_filter, out_grad):
    projected, halo, g, fo = gather_project(in_proj, features)
    mixed, filter_grad, pd, tp = middle(projected, halo, short_taps.T, out_grad, long_filter)
    proj_grad, feat_grad, taps_grad = reduce_grads(pd, features, fo, g, tp)
    return mixed, feat_grad, filter_grad, taps_grad[0:3], proj_grad


def solution(mesh):
    tokens = P(None, AXES)
    rows = P(AXES, None)
    return jax.shard_map(
        local,
        mesh=mesh,
        in_specs=(tokens, rows, P(), tokens, tokens),
        out_specs=(tokens, tokens, tokens, P(), rows),
        check_vma=False,
    )
```

time: 1130 us -> 191 us (0.17)
  blocking collectives: 450 us -> 0 us
  waiting for transfers between devices: 353 us -> 0 us
  Pallas kernels: 0 us -> 177 us
  starting transfers between devices: 156 us -> 0 us
  matrix products: 64.6 us -> 0 us
  local copies, waits for them, and re-layouts: 75.8 us -> 12.4 us
  between operations: 15.8 us -> 0.71 us
    unnamed x1 -> x0, blocking collectives: 386 us -> none
    all_gather x1 -> x0, waiting for transfers between devices: 293 us -> none  [local(): whole_proj = lax.all_gather(in_proj, ('narrow', 'wide'), axis=0, tiled=True)]
    pallas_call x0 -> x3, Pallas kernels: none -> 177 us  [the longest x1 86.6 us: middle(): pl.pallas_call(middle_kernel, out_shape=(jax.ShapeDtypeStruct((256, 128),...]
    unnamed x32 -> x0, starting transfers between devices: 103 us -> none
    dot_general x39 -> x0, matrix products: 64.6 us -> none  [the longest x3 6.43 us: forward_spectrum(): jnp.einsum('cfm,mk->cfk', imag_b, sin_m, precision=HIGH)]
    psum x1 -> x0, blocking collectives: 64.5 us -> none  [local(): taps_grad = lax.psum(taps_part, ('narrow', 'wide'))]
    unnamed x76 -> x19, local copies, waits for them, and re-layouts: 72.3 us -> 11.1 us
    all_to_all x6 -> x0, starting transfers between devices: 49.2 us -> none  [the longest x1 12.8 us: local(): lax.all_to_all(conv_grad, ('narrow', 'wide'), split_axis=0, concat_axis=1...]
  transfers between devices with their start and end apart: 41 -> 0, of which waited for: 8 -> 0; matrix products, arithmetic and copies ran while one was open for 3% -> 0% of each run, Pallas kernels for 0% -> 0%
where the time goes in v1:
time: 191 us; the launch traced here: 190 us
  Pallas kernels  177 us (93%)
  local copies, waits for them, and re-layouts  12.4 us (6%)
    pallas_call x1, Pallas kernels, middle(): pl.pallas_call(middle_kernel, out_shape=(jax.ShapeDtypeStruct((256, 128),...  86.6 us
    pallas_call x1, Pallas kernels, gather_project(): pl.pallas_call(gather_kernel, out_shape=(jax.ShapeDtypeStruct((768, 128),...  46.5 us
    pallas_call x1, Pallas kernels, reduce_grads(): pl.pallas_call(reduce_kernel, out_shape=(jax.ShapeDtypeStruct((6, 4096),...  44.2 us
    unnamed x19, local copies, waits for them, and re-layouts  11.1 us

profile of v1, /device:TPU:0, one launch (start us, length us, event | category | flops | bytes accessed | tf_op | source)
XLA Modules:
  0.0 190.5 jit_solution(17297280269640601540)
XLA Ops:
  0.6 0.9 copy.10
  1.5 0.0 copy-start
  1.5 1.2 copy-done
  2.8 0.0 copy-start.3
  2.8 0.8 copy-done.3
  3.6 46.5 %gather_project.1 = (f32[768,128]{1,0:T(8,128)S(1)}, f32[768,128]{1,0:T(8,128)S(1)}, bf16[3,2,4,4,4,16,512]{6,5,4,3,2,1,0:T(8,128)(2,1)}, bf16[4096,128]{1,0:T(8,128)(2,1)S(1)}) custom-call(bf16[6,4096]{1,0:T(8,128)(2,1)S(1)} %copy-done.3, bf16[4096,128]{1,0:T(8,128)(2,1)S(1)} %copy-done), custom_call_target="tpu_custom_call" | custom-call | tf_op jit(solution)/shard_map/gather_project/pallas_call | solution.py:233
  50.1 0.0 copy-start.1
  50.2 0.0 copy-start.4
  50.2 0.9 copy-done.4
  51.1 0.0 copy-start.5
  51.1 0.8 copy-done.5
  51.9 86.6 %middle.1 = (bf16[256,128]{1,0:T(8,128)(2,1)S(1)}, bf16[256,128]{1,0:T(8,128)(2,1)S(1)}, bf16[768,128]{1,0:T(8,128)(2,1)S(1)}, f32[8,768]{1,0:T(8,128)S(1)}) custom-call(f32[768,128]{1,0:T(8,128)S(1)} %get-tuple-element.16.p_ref, f32[768,128]{1,0:T(8,128)S(1)} %get-tuple-element.17.halo_ref, f32[768,3]{1,0:T(8,128)S(1)} %bitcast.1, ...), custom_call_target="tpu_custom_call" | custom-call | tf_op jit(solution)/shard_map/middle/pallas_call | solution.py:653
  138.6 0.0 copy-done.1
  138.6 0.0 copy-start.2
  138.6 0.7 copy-done.2
  139.3 0.0 copy-start.6
  139.3 0.6 copy-done.6
  139.9 44.2 %reduce_grads.1 = (f32[6,4096]{1,0:T(8,128)}, bf16[4096,128]{1,0:T(8,128)(2,1)}, f32[8,768]{1,0:T(8,128)}) custom-call(bf16[768,128]{1,0:T(8,128)(2,1)} %copy-done.2, bf16[4096,128]{1,0:T(8,128)(2,1)} %feat_ref.3, bf16[4096,128]{1,0:T(8,128)(2,1)} %copy-done.1, bf16[3,2,4,4,4,16,512]{6,5,4,3,2,1,0:T(8,128)(2,1)} %get-tuple-element.21.g_ref, f32[8,768]{1,0:T(8,128)} %copy-done.6), custom_call_target="tpu_custom_call" | custom-call | tf_op jit(solution)/shard_map/reduce_grads/pallas_call | solution.py:449
  184.0 1.3 slice.3
  185.4 0.6 copy.15
  186.0 2.3 %copy.16 = bf16[4096,128]{1,0:T(8,128)(2,1)} copy(bf16[4096,128]{1,0:T(8,128)(2,1)} %get-tuple-element.33) | data formatting | bytes 2097152
  188.3 0.6 copy.17
  188.9 1.6 copy.18
Async XLA Ops:
  1.5 1.2 copy-start
  2.8 0.8 copy-start.3
  50.1 88.4 %copy-start.1 = (bf16[4096,128]{1,0:T(8,128)(2,1)}, bf16[4096,128]{1,0:T(8,128)(2,1)S(1)}, u32[]{:S(2)}) copy-start(bf16[4096,128]{1,0:T(8,128)(2,1)S(1)} %get-tuple-element.20.fo_ref) | copy-start | bytes 3145732
  50.2 0.9 copy-start.4
  51.1 0.8 copy-start.5
  138.6 0.7 copy-start.2
  139.3 0.6 copy-start.6

commit v2 on v0

v2 whole, which is shorter than its diff:
```python
import math

import jax
import jax.numpy as jnp
from jax import lax
from jax.experimental import pallas as pl
from jax.experimental.pallas import tpu as pltpu
from jax.sharding import PartitionSpec as P

MESH = pl.DeviceIdType.MESH
BF = jnp.bfloat16
F32 = jnp.float32
ORDERS = (("x", "y", "z"), ("y", "z", "x"), ("z", "x", "y"))
AXES = ("narrow", "wide")


def place(pos):
    y = pos["y"]
    return (pos["z"] * 4 + lax.rem(y, 2) * 2 + pos["c"], (y // 2) * 4 + pos["x"])


def position():
    n = lax.axis_index("narrow")
    w = lax.axis_index("wide")
    pos = {
        "x": lax.rem(w, 4),
        "y": (w // 4) * 2 + lax.rem(n // 2, 2),
        "z": n // 4,
        "c": lax.rem(n, 2),
    }
    return n, w, pos


def shifted(pos, axis, by):
    other = dict(pos)
    other[axis] = lax.rem(pos[axis] + by + 4, 4)
    return place(other)


def other_core(pos):
    other = dict(pos)
    other["c"] = 1 - pos["c"]
    return place(other)


def shard_id(s):
    return (s // 8, lax.rem(s, 8))


def remote(src, dst, send, recv, device):
    return pltpu.make_async_remote_copy(
        src_ref=src, dst_ref=dst, send_sem=send, recv_sem=recv, device_id=device, device_id_type=MESH
    )


def greet(devices):
    barrier = pltpu.get_barrier_semaphore()
    for device in devices:
        pl.semaphore_signal(barrier, inc=1, device_id=device, device_id_type=MESH)
    pl.semaphore_wait(barrier, len(devices))


def piece_index(cls, z, yh, yl, x):
    at = {"x": x, "y": yh * 2 + yl, "z": z}
    d0, d1, d2 = ORDERS[cls]
    return (at[d2], at[d1], at[d0])


def dims(a, b):
    return (((a,), (b,)), ((), ()))


def lanes(rows):
    return lax.broadcasted_iota(jnp.int32, (rows, 128), 1)


def one_hot(rows, cols, test):
    r = lax.broadcasted_iota(jnp.int32, (rows, cols), 0)
    c = lax.broadcasted_iota(jnp.int32, (rows, cols), 1)
    return jnp.where(test(r, c), 1.0, 0.0).astype(BF)


def wide_block(g_ref, cls, yh, x):
    parts = []
    for z in range(4):
        for yl in range(2):
            for core in range(2):
                i2, i1, i0 = piece_index(cls, z, yh, yl, x)
                parts.append(g_ref[cls, core, i2, i1, i0])
    return jnp.concatenate(parts, axis=0)


def half(ref, phase, k):
    if phase == 0:
        return ref.at[:, pl.ds(k * 256, 256)]
    return ref.at[pl.ds(k * 2, 2)]


def build_toeplitz(tt, h_ref, ch):
    lane = lanes(128)
    row = lax.broadcasted_iota(jnp.int32, (128, 128), 0)
    upper = lane >= row

    def rolled(k):
        taps = jnp.broadcast_to(h_ref[ch, pl.ds(k, 1), :], (128, 128))
        return pltpu.roll(taps, 0, 1, stride=1, stride_axis=0)

    @pl.loop(0, 8)
    def _(g):
        prev = jnp.where(g > 0, rolled(jnp.maximum(16 * g - 1, 0)), 0.0)
        at = pl.ds(pl.multiple_of(g * 128, 128), 128)
        for i in range(16):
            cur = rolled(16 * g + i)
            tt[at, i * 128 : (i + 1) * 128] = jnp.where(upper, cur, prev).astype(BF)
            prev = cur


def spread_blocks(xs, col, x):
    lane = lanes(128)
    for i in range(16):
        moved = pltpu.roll(x, i, 1) if i else x
        xs[i * 128 : (i + 1) * 128, col * 128 : (col + 1) * 128] = jnp.where(lane < i, 0.0, moved).astype(BF)


def toeplitz_product(tt, xs, cols):
    lane = lanes(128)
    out = jnp.dot(tt[...], xs[:, 0 : cols * 128], preferred_element_type=F32)
    results = []
    for c in range(cols):
        at = slice(c * 128, (c + 1) * 128)
        acc = out[896:1024, at]
        for g in range(6, -1, -1):
            acc = jnp.where(lane < 16, 0.0, pltpu.roll(acc, 16, 1)) + out[g * 128 : (g + 1) * 128, at]
        results.append(acc.astype(BF))
    return results


def hyena_kernel(
    proj_hbm, feat_hbm, taps_hbm, og_hbm, lf_hbm,
    mixed_ref, fgrad_ref, fgout_ref, tout_ref, grad_ref,
    proj_ref, feat_ref, taps_ref, og_ref, lf_ref,
    stage, land, blk, rows, hland, fh, g_ref, fo_ref, p_ref, halo_ref, tcol,
    rowbuf, send_f, land_f, send_a, land_a, send_b, land_b, send_c, land_c,
    ogn, hf, gf, feat, featn, tt0, tt1, xs, xc, pd_ref,
    pdo, pdc, p, ra3, rb3, rc3, rd3, ra2, rb2, rc2, rd2, ra1, rb1, rc1, rd1,
    stage2, land2, tl,
    ins, s0, r0, ss, rs, ds, dr, hs, hr, fs, fr, xsend, xrecv, os, orr,
    ps, pr, ss2, rs2, s02, r02, tsn, trc, near,
):
    n, w, pos = position()
    c = pos["c"]
    s = n * 8 + w
    right_shard = shard_id(lax.rem(s + 1, 128))
    left_shard = shard_id(lax.rem(s + 127, 128))
    wide_peers = [(n, lax.rem(w + i, 8)) for i in range(1, 8)]
    line = {a: [shifted(pos, a, d) for d in (1, 2, 3)] for a in "xyz"}
    core = other_core(pos)
    copies = [
        pltpu.make_async_copy(a, b, ins.at[k])
        for k, (a, b) in enumerate(
            ((proj_hbm, proj_ref), (feat_hbm, feat_ref), (taps_hbm, taps_ref), (og_hbm, og_ref), (lf_hbm, lf_ref))
        )
    ]
    for cp in copies:
        cp.start()
    barrier = pltpu.get_barrier_semaphore()
    greeted = wide_peers + line["y"] + line["z"] + [core, right_shard, left_shard]
    for device in greeted:
        pl.semaphore_signal(barrier, inc=1, device_id=device, device_id_type=MESH)
    copies[0].wait()
    for q in range(8):
        stage[q, 0:6, :] = proj_ref[:, q * 512 : (q + 1) * 512].astype(F32)
        stage[q, 6:8, :] = jnp.zeros((2, 512), F32)
    pl.semaphore_wait(barrier, len(greeted))

    def tell(k, devices):
        for device in devices:
            pl.semaphore_signal(near.at[k], inc=1, device_id=device, device_id_type=MESH)

    started = []

    def push(src, dst, a, b, device):
        cp = remote(src, dst, a, b, device)
        cp.start()
        started.append(cp)
        return cp

    first = []
    for i in range(1, 8):
        q = lax.rem(w + i, 8)
        first.append(push(stage.at[q], land.at[w], s0.at[i], r0.at[i], (n, q)))
    tell(0, line["x"])
    land[w] = stage[w]
    for cp in first:
        cp.wait_recv()
    for q in range(8):
        blk[q * 6 : (q + 1) * 6, :] = land[q, 0:6, :]

    index = [[pos[a] for a in reversed(order)] for order in ORDERS]
    for cls in range(3):
        i2, i1, i0 = index[cls]
        g_ref[cls, c, i2, i1, i0] = blk[cls * 16 : (cls + 1) * 16, :].astype(BF)

    def unit(ref, cls, phase, j):
        i2, i1, _ = index[cls]
        if phase == 0:
            return ref.at[i2, i1, j]
        if phase == 1:
            return ref.at[i2, j]
        return ref.at[j]

    d2d = []

    def cross(cls, j, k):
        ref = g_ref.at[cls, c, j]
        d2d.append(push(ref, ref, ds.at[cls, k], dr.at[cls, k], core))

    def exchange(src, dst, k):
        ww = [lax.rem(w + j, 8) for j in range(8)]
        for j in range(1, 8):
            remote(src.at[n * 8 + ww[j]], dst.at[s], xsend.at[k], xrecv.at[k], (n, ww[j])).start()

        @pl.loop(1, 16)
        def _(i):
            nn = lax.rem(n + i, 16)
            for j in range(8):
                remote(src.at[nn * 8 + ww[j]], dst.at[s], xsend.at[k], xrecv.at[k], (nn, ww[j])).start()

        dst[s] = src[s]
        whole = pl.ds(0, 127)
        cp = remote(src.at[whole], dst.at[whole], xsend.at[k], xrecv.at[k], (n, w))
        started.append(cp)
        return cp

    def pack(buf, parts):
        for r, value in parts.items():
            rowbuf[pl.ds(r, 128, stride=8), :] = value
        buf[...] = rowbuf[...].reshape(128, 8, 128).astype(BF)

    def unpack(buf):
        rowbuf[...] = buf[...].astype(F32).reshape(1024, 128)

    def plane(r):
        return rowbuf[pl.ds(r, 128, stride=8), :]

    fcp = lfx = None
    for phase in range(3):
        legs = []
        for cls in range(3):
            axis = ORDERS[cls][phase]
            i = pos[axis]
            right, left = shifted(pos, axis, 1), shifted(pos, axis, -1)
            mine = unit(g_ref.at[cls, c], cls, phase, i)
            a = push(mine, mine, ss.at[cls, phase, 0], rs.at[cls, phase, 0], right)
            b = push(mine, mine, ss.at[cls, phase, 1], rs.at[cls, phase, 1], left)
            legs.append((a, b, right, left, i))
            if phase == 2:
                cross(cls, i, 0)
        if phase == 0:
            copies[1].wait()
            sel = one_hot(
                16, 128, lambda r, l: ((r < 2) & (l == r + 126)) | ((r >= 2) & (r < 4) & (l == r - 2))
            )
            rows[...] = lax.dot_general(
                sel, feat_ref[...], dims(1, 1), preferred_element_type=F32
            ).astype(BF)
            ha = push(rows, hland.at[0], hs.at[0], hr.at[0], right_shard)
            hb = push(rows, hland.at[1], hs.at[1], hr.at[1], left_shard)
            fcp = push(feat_ref, fo_ref, fs, fr, core)
            pl.semaphore_wait(near.at[0], 3)
            tell(1, line["y"])
        if phase == 1:
            fh[:, 0:128] = feat_ref[...]
            pl.semaphore_wait(near.at[1], 3)
            tell(2, [core])
            for k in range(2, 5):
                copies[k].wait()
            lf = lf_ref[...].astype(F32)
            zero = jnp.zeros((128, 128), F32)
            pack(send_f, {0: lf[0:128], 1: lf[128:256], **{r: zero for r in range(2, 8)}})
            ocp = push(og_ref, ogn, os, orr, left_shard)
            tc = jnp.concatenate([taps_ref[...], jnp.zeros((125, 768), F32)], axis=0)
            for k in range(6):
                tcol[k * 128 : (k + 1) * 128, :] = tc[:, k * 128 : (k + 1) * 128].T
        if phase == 2:
            pl.semaphore_wait(near.at[2], 1)
            lfx = exchange(send_f, land_f, 0)
            ha.wait_recv()
            hb.wait_recv()
            row = lax.broadcasted_iota(jnp.int32, (16, 4096), 0)
            both = jnp.where(row < 2, hland[0].astype(F32), hland[1].astype(F32)).astype(BF)
            lo = jnp.where(s > 0, 0, 2)
            hi = jnp.where(s < 127, 4, 2)
            spread = one_hot(16, 128, lambda r, l: (r == l) & (r >= lo) & (r < hi))
            fh[:, 128:256] = lax.dot_general(
                both, spread, dims(0, 0), preferred_element_type=F32
            ).astype(BF)
        second = []
        for cls in range(3):
            a, b, right, left, i = legs[cls]
            a.wait_recv()
            got = half(unit(g_ref.at[cls, c], cls, phase, lax.rem(i + 3, 4)), phase, 0)
            e = push(got, got, ss.at[cls, phase, 2], rs.at[cls, phase, 2], right)
            b.wait_recv()
            got = half(unit(g_ref.at[cls, c], cls, phase, lax.rem(i + 1, 4)), phase, 1)
            f = push(got, got, ss.at[cls, phase, 3], rs.at[cls, phase, 3], left)
            second.append((e, f))
            if phase == 2:
                cross(cls, lax.rem(i + 3, 4), 1)
                cross(cls, lax.rem(i + 1, 4), 2)
        if phase == 2:
            lfx.wait_recv()
            unpack(land_f)
            for ch in range(2):
                hf[ch] = plane(ch)
            build_toeplitz(tt0, hf, 0)
            build_toeplitz(tt1, hf, 1)
        for cls in range(3):
            e, f = second[cls]
            e.wait_recv()
            f.wait_recv()
            if phase == 2:
                cross(cls, lax.rem(legs[cls][4] + 2, 4), 3)
    for cp in d2d:
        cp.wait_recv()

    for cls in range(3):
        acc = None
        for q in range(8):
            lhs = wide_block(g_ref, cls, q // 4, q % 4)
            term = jnp.dot(lhs, fh[q * 512 : (q + 1) * 512, :], preferred_element_type=F32)
            acc = term if acc is None else acc + term
        for m in range(16):
            at = slice(m * 48 + cls * 16, m * 48 + cls * 16 + 16)
            p_ref[at, :] = acc[m * 16 : (m + 1) * 16, 0:128]
            halo_ref[at, :] = acc[m * 16 : (m + 1) * 16, 128:256]

    lane = lanes(256)
    for part in range(3):
        at = slice(part * 256, (part + 1) * 256)
        v = p_ref[at, :]
        halo = halo_ref[at, :]
        t0, t1, t2 = tcol[at, 0:1], tcol[at, 1:2], tcol[at, 2:3]
        v1 = jnp.where(lane < 1, pltpu.roll(halo, 127, 1), pltpu.roll(v, 1, 1))
        v2 = jnp.where(lane < 2, halo, pltpu.roll(v, 2, 1))
        feat[part] = t0 * v + t1 * v1 + t2 * v2
        n1 = jnp.where(lane < 1, pltpu.roll(v, 1, 1), pltpu.roll(halo, 127, 1))
        featn[part] = t0 * pltpu.roll(halo, 126, 1) + t1 * n1 + t2 * pltpu.roll(v, 2, 1)
    og = og_ref[...].astype(F32)
    gated = feat[1] * feat[2]
    cot = og * feat[0]
    pack(send_a, {0: gated[0:128], 1: gated[128:256], 2: cot[0:128], 3: cot[128:256]})
    go = exchange(send_a, land_a, 1)
    go.wait_recv()
    unpack(land_a)

    anti = one_hot(128, 128, lambda r, l: r + l == 127)
    row = lax.broadcasted_iota(jnp.int32, (128, 128), 0)
    lane1 = lanes(128)
    ahead = jnp.zeros((128, 128), F32)
    cots = []
    for ch in range(2):
        gf[ch] = plane(ch)
        cots.append(plane(2 + ch).astype(BF))
    for ch in range(2):
        xg = lax.dot_general(anti, gf[ch].astype(BF), dims(1, 1), preferred_element_type=F32)
        back = lax.dot_general(cots[ch], anti, dims(0, 0), preferred_element_type=F32)
        spread_blocks(xs, 1, xg)
        spread_blocks(xs, 0, back)
        xc[ch] = xs[:, 0:128]
        yc, yg = toeplitz_product(tt0 if ch == 0 else tt1, xs, 2)
        conv = lax.dot_general(yg, anti, dims(0, 0), preferred_element_type=F32)
        gg = lax.dot_general(anti, yc, dims(1, 1), preferred_element_type=F32)
        rowbuf[pl.ds(ch, 128, stride=8), :] = conv
        rowbuf[pl.ds(2 + ch, 128, stride=8), :] = gg
        for k, value in ((ch, conv), (2 + ch, gg)):
            nxt = jnp.where(row < 127, pltpu.roll(value, 127, 0), 0.0)
            moved = pltpu.roll(nxt, 2 * k, 1) if k else nxt
            ahead = jnp.where((lane1 >= 2 * k) & (lane1 < 2 * k + 2), moved, ahead)
    pack(send_b, {4: ahead})
    ret = exchange(send_b, land_b, 2)
    build_toeplitz(tt0, gf, 0)
    build_toeplitz(tt1, gf, 1)
    ocp.wait_recv()
    ret.wait_recv()
    unpack(land_b)

    def channels(r):
        return jnp.concatenate([plane(r), plane(r + 1)], axis=0)

    conv, gg = channels(0), channels(2)
    ahead = plane(4)
    convn = jnp.concatenate([ahead, pltpu.roll(ahead, 126, 1)], axis=0)
    ggn = jnp.concatenate([pltpu.roll(ahead, 124, 1), pltpu.roll(ahead, 122, 1)], axis=0)
    mixed_ref[...] = (feat[0] * conv).astype(BF)
    ogv = ogn[...].astype(F32)
    last = s == 127

    def derivative(part):
        if part == 0:
            return og * conv
        return gg * feat[3 - part]

    for part in range(3):
        at = slice(part * 256, (part + 1) * 256)
        fd = derivative(part)
        fdn = ogv * convn if part == 0 else ggn * featn[3 - part]
        fdn = jnp.where(last, 0.0, fdn)
        t0, t1, t2 = tcol[at, 0:1], tcol[at, 1:2], tcol[at, 2:3]
        f1 = jnp.where(lane < 127, pltpu.roll(fd, 127, 1), pltpu.roll(fdn, 127, 1))
        f2 = jnp.where(lane < 126, pltpu.roll(fd, 126, 1), pltpu.roll(fdn, 126, 1))
        pd_ref[at, :] = (t0 * fd + t1 * f1 + t2 * f2).astype(BF)
    pcp = push(pd_ref, pdo, ps, pr, core)

    for part in range(3):
        at = slice(part * 256, (part + 1) * 256)
        fd = derivative(part)
        v = p_ref[at, :]
        halo = halo_ref[at, :]
        v1 = jnp.where(lane < 1, pltpu.roll(halo, 127, 1), pltpu.roll(v, 1, 1))
        v2 = jnp.where(lane < 2, halo, pltpu.roll(v, 2, 1))
        total = jnp.zeros((256, 128), F32)
        for k, q in enumerate((v, v1, v2)):
            total = jnp.where(lane == k, jnp.sum(fd * q, axis=1, keepdims=True), total)
        tl[0, c, :, at] = total.T[0:8, :]

    def tap_send(k, peers, slot):
        return [
            push(tl.at[k, slot], tl.at[k, slot], tsn.at[k, i], trc.at[k, i], device)
            for i, device in enumerate(peers)
        ]

    def tap_sum(k, cps, count):
        for cp in cps:
            cp.wait_recv()
        total = tl[k, 0]
        for i in range(1, count):
            total = total + tl[k, i]
        return total

    tcp = tap_send(0, [core], c)
    fcp.wait_recv()
    pcp.wait_recv()
    for cls in range(3):
        for z in range(4):
            for yl in range(2):
                at = pl.ds(pl.multiple_of((z * 4 + yl * 2 + c) * 48 + cls * 16, 16), 16)
                to = cls * 128 + z * 32 + yl * 16
                pdc[to : to + 16, 0:128] = pd_ref[at, :]
                pdc[to : to + 16, 128:256] = pdo[at, :]

    for yh in range(2):
        for x in range(4):
            cols = slice((yh * 4 + x) * 512, (yh * 4 + x + 1) * 512)
            rhs = jnp.concatenate([feat_ref[cols, :], fo_ref[cols, :]], axis=1)
            for cls in range(3):
                part = lax.dot_general(
                    pdc[cls * 128 : (cls + 1) * 128, :], rhs, dims(1, 1), preferred_element_type=F32
                ).astype(BF)
                for z in range(4):
                    for yl in range(2):
                        i2, i1, i0 = piece_index(cls, z, yh, yl, x)
                        k = z * 32 + yl * 16
                        p[cls, i2, i1, i0] = part[k : k + 16, :]

    bufs = {2: (ra3, rb3, rc3, rd3), 1: (ra2, rb2, rc2, rd2), 0: (ra1, rb1, rc1, rd1)}

    def add(dst, src):
        dst[...] = (dst[...].astype(F32) + src[...].astype(F32)).astype(BF)

    def feat_part(qs):
        for q in qs:
            total = None
            for cls in range(3):
                lhs = jnp.concatenate(
                    [pd_ref[m * 48 + cls * 16 : m * 48 + cls * 16 + 16, :] for m in range(16)], axis=0
                )
                term = lax.dot_general(
                    lhs, wide_block(g_ref, cls, q // 4, q % 4), dims(0, 0), preferred_element_type=F32
                )
                total = term if total is None else total + term
            fgrad_ref[q * 512 : (q + 1) * 512, :] = total.T.astype(BF)

    fgx = None
    for phase in (2, 1, 0):
        ra, rb, rc, rd = bufs[phase]
        legs = []
        for cls in range(3):
            axis = ORDERS[cls][phase]
            i = pos[axis]
            right, left = shifted(pos, axis, 1), shifted(pos, axis, -1)
            far, up, down = (unit(p.at[cls], cls, phase, lax.rem(i + d, 4)) for d in (2, 1, 3))
            sem = [(ss2.at[cls, phase, k], rs2.at[cls, phase, k]) for k in range(6)]
            a = push(half(far, phase, 0), ra.at[cls], *sem[0], right)
            b = push(half(far, phase, 1), rb.at[cls], *sem[1], left)
            d = push(half(up, phase, 1), half(rc.at[cls], phase, 1), *sem[2], right)
            e = push(half(down, phase, 0), half(rd.at[cls], phase, 0), *sem[3], left)
            legs.append((sem, a, b, d, e, up, down, right, left, i))
        if phase == 2:
            feat_part(range(2))
        if phase == 1:
            feat_part(range(5, 7))
        if phase == 0:
            feat_part(range(7, 8))
        more = []
        for cls in range(3):
            sem, a, b, d, e, up, down, right, left, i = legs[cls]
            a.wait_recv()
            add(half(up, phase, 0), ra.at[cls])
            f = push(half(up, phase, 0), half(rc.at[cls], phase, 0), *sem[4], right)
            b.wait_recv()
            add(half(down, phase, 1), rb.at[cls])
            g = push(half(down, phase, 1), half(rd.at[cls], phase, 1), *sem[5], left)
            more.append((f, g))
        if phase == 2:
            tl[1, pos["x"]] = tap_sum(0, tcp, 2)
            tcp = tap_send(1, line["x"], pos["x"])
            for ch in range(2):
                (y,) = toeplitz_product(tt0 if ch == 0 else tt1, xc.at[ch], 1)
                rowbuf[pl.ds(ch, 128, stride=8), :] = lax.dot_general(
                    anti, y, dims(1, 1), preferred_element_type=F32
                )
            pack(send_c, {})
            fgx = exchange(send_c, land_c, 3)
            feat_part(range(2, 5))
        if phase == 1:
            tl[2, pos["y"]] = tap_sum(1, tcp, 4)
            tcp = tap_send(2, line["y"], pos["y"])
        if phase == 0:
            tl[3, pos["z"]] = tap_sum(2, tcp, 4)
            tcp = tap_send(3, line["z"], pos["z"])
        for cls in range(3):
            sem, a, b, d, e, up, down, right, left, i = legs[cls]
            for k in (d, e) + more[cls]:
                k.wait_recv()
            mine = unit(p.at[cls], cls, phase, i)
            total = mine[...].astype(F32) + rc[cls].astype(F32) + rd[cls].astype(F32)
            if phase == 0:
                blk[cls * 16 : (cls + 1) * 16, :] = total
            else:
                mine[...] = total.astype(BF)

    for q in range(8):
        stage2[q, 0:6, :] = blk[q * 6 : (q + 1) * 6, :]
        stage2[q, 6:8, :] = jnp.zeros((2, 512), F32)
    final = []
    for i in range(1, 8):
        q = lax.rem(w + i, 8)
        final.append(push(stage2.at[q], land2.at[w], s02.at[i], r02.at[i], (n, q)))
    land2[w] = stage2[w]
    tout_ref[...] = tap_sum(3, tcp, 4)[0:3]
    fgx.wait_recv()
    unpack(land_c)
    fgout_ref[...] = channels(0).astype(BF)
    for cp in final:
        cp.wait_recv()
    for q in range(8):
        grad_ref[:, q * 512 : (q + 1) * 512] = land2[q, 0:6, :]
    for cp in started:
        cp.wait_send()


VM = pl.BlockSpec(memory_space=pltpu.VMEM)
ANY = pl.BlockSpec(memory_space=pl.ANY)


def hyena(in_proj, features, taps, out_grad, long_filter):
    sem = pltpu.SemaphoreType.DMA
    vm = pltpu.VMEM
    tile = (128, 8, 128)
    return pl.pallas_call(
        hyena_kernel,
        out_shape=(
            jax.ShapeDtypeStruct((256, 128), BF),
            jax.ShapeDtypeStruct((4096, 128), BF),
            jax.ShapeDtypeStruct((256, 128), BF),
            jax.ShapeDtypeStruct((3, 768), F32),
            jax.ShapeDtypeStruct((6, 4096), F32),
        ),
        in_specs=[ANY] * 5,
        out_specs=(VM,) * 5,
        scratch_shapes=[
            vm((6, 4096), BF), vm((4096, 128), BF), vm((3, 768), F32), vm((256, 128), BF), vm((256, 128), BF),
            vm((8, 8, 512), F32), vm((8, 8, 512), F32), vm((48, 512), F32),
            vm((16, 4096), BF), vm((2, 16, 4096), BF), vm((4096, 256), BF),
            vm((3, 2, 4, 4, 4, 16, 512), BF), vm((4096, 128), BF),
            vm((768, 128), F32), vm((768, 128), F32), vm((768, 128), F32),
            vm((1024, 128), F32),
        ]
        + [vm(tile, BF)] * 8
        + [
            vm((256, 128), BF), vm((2, 128, 128), F32), vm((2, 128, 128), F32),
            vm((3, 256, 128), F32), vm((3, 256, 128), F32),
            vm((1024, 2048), BF), vm((1024, 2048), BF), vm((2048, 256), BF), vm((2, 2048, 128), BF),
            vm((768, 128), BF),
            vm((768, 128), BF), vm((384, 256), BF), vm((3, 4, 4, 4, 16, 512), BF),
            vm((3, 2, 4, 16, 512), BF), vm((3, 2, 4, 16, 512), BF),
            vm((3, 4, 4, 16, 512), BF), vm((3, 4, 4, 16, 512), BF),
            vm((3, 2, 16, 512), BF), vm((3, 2, 16, 512), BF),
            vm((3, 4, 16, 512), BF), vm((3, 4, 16, 512), BF),
            vm((3, 16, 256), BF), vm((3, 16, 256), BF),
            vm((3, 16, 512), BF), vm((3, 16, 512), BF),
            vm((8, 8, 512), F32), vm((8, 8, 512), F32), vm((4, 4, 8, 768), F32),
            sem((5,)), sem((8,)), sem((8,)),
            sem((3, 3, 4)), sem((3, 3, 4)), sem((3, 4)), sem((3, 4)),
            sem((2,)), sem((2,)), sem, sem, sem((4,)), sem((4,)), sem, sem,
            sem, sem, sem((3, 3, 6)), sem((3, 3, 6)), sem((8,)), sem((8,)), sem((4, 3)), sem((4, 3)),
            pltpu.SemaphoreType.REGULAR((3,)),
        ],
        compiler_params=pltpu.CompilerParams(
            collective_id=1, has_side_effects=True, vmem_limit_bytes=58 * 1024 * 1024
        ),
        name="hyena",
    )(in_proj, features, taps, out_grad, long_filter)


def local(features, in_proj, short_taps, long_filter, out_grad):
    return hyena(in_proj, features, short_taps, out_grad, long_filter)


def solution(mesh):
    tokens = P(None, AXES)
    rows = P(AXES, None)
    return jax.shard_map(
        local,
        mesh=mesh,
        in_specs=(tokens, rows, P(), tokens, tokens),
        out_specs=(tokens, tokens, tokens, P(), rows),
        check_vma=False,
    )
```

time: 1130 us -> 118 us (0.10)
  blocking collectives: 450 us -> 0 us
  waiting for transfers between devices: 353 us -> 0 us
  starting transfers between devices: 156 us -> 0 us
  Pallas kernels: 0 us -> 111 us
  local copies, waits for them, and re-layouts: 75.8 us -> 5.66 us
  matrix products: 64.6 us -> 0 us
  between operations: 15.8 us -> 0.65 us
    unnamed x1 -> x0, blocking collectives: 386 us -> none
    all_gather x1 -> x0, waiting for transfers between devices: 293 us -> none  [local(): whole_proj = lax.all_gather(in_proj, ('narrow', 'wide'), axis=0, tiled=True)]
    pallas_call x0 -> x1, Pallas kernels: none -> 111 us  [hyena(): pl.pallas_call(hyena_kernel, out_shape=(jax.ShapeDtypeStruct((256, 128),...]
    unnamed x32 -> x0, starting transfers between devices: 103 us -> none
    unnamed x76 -> x11, local copies, waits for them, and re-layouts: 72.3 us -> 5.66 us
    dot_general x39 -> x0, matrix products: 64.6 us -> none  [the longest x3 6.43 us: forward_spectrum(): jnp.einsum('cfm,mk->cfk', imag_b, sin_m, precision=HIGH)]
    psum x1 -> x0, blocking collectives: 64.5 us -> none  [local(): taps_grad = lax.psum(taps_part, ('narrow', 'wide'))]
    all_to_all x6 -> x0, starting transfers between devices: 49.2 us -> none  [the longest x1 12.8 us: local(): lax.all_to_all(conv_grad, ('narrow', 'wide'), split_axis=0, concat_axis=1...]
  transfers between devices with their start and end apart: 41 -> 0, of which waited for: 8 -> 0; matrix products, arithmetic and copies ran while one was open for 3% -> 0% of each run, Pallas kernels for 0% -> 0%
where the time goes in v2:
time: 118 us; the launch traced here: 117 us
  Pallas kernels  111 us (94%)
  local copies, waits for them, and re-layouts  5.66 us (5%)
    pallas_call x1, Pallas kernels, hyena(): pl.pallas_call(hyena_kernel, out_shape=(jax.ShapeDtypeStruct((256, 128),...  111 us
    unnamed x11, local copies, waits for them, and re-layouts  5.66 us

profile of v2, /device:TPU:0, one launch (start us, length us, event | category | flops | bytes accessed | tf_op | source)
XLA Modules:
  0.0 117.3 jit_solution(6636699144378436868)
XLA Ops:
  0.6 111.0 %hyena.1 = (bf16[256,128]{1,0:T(8,128)(2,1)}, bf16[4096,128]{1,0:T(8,128)(2,1)}, bf16[256,128]{1,0:T(8,128)(2,1)}, f32[3,768]{1,0:T(4,128)}, f32[6,4096]{1,0:T(8,128)}) custom-call(bf16[6,4096]{1,0:T(8,128)(2,1)} %proj_hbm.1, bf16[4096,128]{1,0:T(8,128)(2,1)} %feat_hbm.1, f32[3,768]{1,0:T(4,128)} %taps_hbm.1, bf16[256,128]{1,0:T(8,128)(2,1)} %og_hbm.1, ...), custom_call_target="tpu_custom_call" | custom-call | tf_op jit(solution)/shard_map/hyena/pallas_call | solution.py:571
  111.7 1.5 %copy.15 = bf16[256,128]{1,0:T(8,128)(2,1)} copy(bf16[256,128]{1,0:T(8,128)(2,1)} %get-tuple-element.10) | data formatting | bytes 131072
  113.1 0.0 copy-start.1
  113.1 0.0 copy-start.2
  113.1 2.3 %copy.16 = bf16[4096,128]{1,0:T(8,128)(2,1)} copy(bf16[4096,128]{1,0:T(8,128)(2,1)} %get-tuple-element.11) | data formatting | bytes 2097152
  115.4 0.0 copy-done.1
  115.4 0.0 copy-start
  115.4 0.6 copy.17
  116.1 0.0 copy-done.2
  116.1 0.6 copy.18
  116.7 0.0 copy-done
  116.7 0.7 copy.19
Async XLA Ops:
  113.1 2.3 %copy-start.1 = (bf16[256,128]{1,0:T(8,128)(2,1)S(1)}, bf16[256,128]{1,0:T(8,128)(2,1)}, u32[]{:S(2)}) copy-start(bf16[256,128]{1,0:T(8,128)(2,1)} %get-tuple-element.12) | copy-start | bytes 196612
  113.1 2.9 %copy-start.2 = (f32[3,768]{1,0:T(4,128)S(1)}, f32[3,768]{1,0:T(4,128)}, u32[]{:S(2)}) copy-start(f32[3,768]{1,0:T(4,128)} %get-tuple-element.13) | copy-start | bytes 27652
  115.4 1.2 %copy-start = (f32[6,4096]{1,0:T(8,128)S(1)}, f32[6,4096]{1,0:T(8,128)}, u32[]{:S(2)}) copy-start(f32[6,4096]{1,0:T(8,128)} %get-tuple-element.14) | copy-start | bytes 294916

commit v3 on v2

--- a/solution.py
+++ b/solution.py
@@ -137,13 +137,14 @@
 
 def hyena_kernel(
     proj_hbm, feat_hbm, taps_hbm, og_hbm, lf_hbm,
-    mixed_ref, fgrad_ref, fgout_ref, tout_ref, grad_ref,
+    mixed_hbm, fgrad_hbm, fgout_hbm, tout_hbm, grad_hbm,
+    mixed_ref, fgrad_ref, fgout_ref, tout_ref, grad_ref, outs,
     proj_ref, feat_ref, taps_ref, og_ref, lf_ref,
     stage, land, blk, rows, hland, fh, g_ref, fo_ref, p_ref, halo_ref, tcol,
     rowbuf, send_f, land_f, send_a, land_a, send_b, land_b, send_c, land_c,
     ogn, hf, gf, feat, featn, tt0, tt1, xs, xc, pd_ref,
     pdo, pdc, p, ra3, rb3, rc3, rd3, ra2, rb2, rc2, rd2, ra1, rb1, rc1, rd1,
-    stage2, land2, tl,
+    stage2, land2, tl, pdt,
     ins, s0, r0, ss, rs, ds, dr, hs, hr, fs, fr, xsend, xrecv, os, orr,
     ps, pr, ss2, rs2, s02, r02, tsn, trc, near,
 ):
@@ -178,6 +179,12 @@
             pl.semaphore_signal(near.at[k], inc=1, device_id=device, device_id_type=MESH)
 
     started = []
+    stores = []
+
+    def store(k, src, dst):
+        cp = pltpu.make_async_copy(src, dst, outs.at[k])
+        cp.start()
+        stores.append(cp)
 
     def push(src, dst, a, b, device):
         cp = remote(src, dst, a, b, device)
@@ -201,14 +208,6 @@
         i2, i1, i0 = index[cls]
         g_ref[cls, c, i2, i1, i0] = blk[cls * 16 : (cls + 1) * 16, :].astype(BF)
 
-    def unit(ref, cls, phase, j):
-        i2, i1, _ = index[cls]
-        if phase == 0:
-            return ref.at[i2, i1, j]
-        if phase == 1:
-            return ref.at[i2, j]
-        return ref.at[j]
-
     d2d = []
 
     def cross(cls, j, k):
@@ -243,84 +242,127 @@
     def plane(r):
         return rowbuf[pl.ds(r, 128, stride=8), :]
 
-    fcp = lfx = None
-    for phase in range(3):
-        legs = []
+    def piece(cls, i2, i1, i0):
+        return g_ref.at[cls, c, i2, i1, i0]
+
+    def row_of(cls, i2, i1):
+        return g_ref.at[cls, c, i2, i1]
+
+    def near_by(cls, phase):
+        axis = ORDERS[cls][phase]
+        return shifted(pos, axis, 1), shifted(pos, axis, -1)
+
+    def ring(cls, phase, k, ref, device):
+        return push(ref, ref, ss.at[cls, phase, k], rs.at[cls, phase, k], device)
+
+    def off(i, d):
+        return lax.rem(i + d, 4)
+
+    legs = []
+    for cls in range(3):
+        i2, i1, i0 = index[cls]
+        right, left = near_by(cls, 0)
+        mine = piece(cls, i2, i1, i0)
+        legs.append((ring(cls, 0, 0, mine, right), ring(cls, 0, 1, mine, left)))
+    pl.semaphore_wait(near.at[0], 3)
+    tell(1, line["y"])
+    copies[1].wait()
+    sel = one_hot(
+        16, 128, lambda r, l: ((r < 2) & (l == r + 126)) | ((r >= 2) & (r < 4) & (l == r - 2))
+    )
+    rows[...] = lax.dot_general(sel, feat_ref[...], dims(1, 1), preferred_element_type=F32).astype(BF)
+    halves = []
+    for cls in range(3):
+        i2, i1, i0 = index[cls]
+        right, left = near_by(cls, 0)
+        legs[cls][0].wait_recv()
+        e = ring(cls, 0, 2, half(piece(cls, i2, i1, off(i0, 3)), 0, 0), right)
+        legs[cls][1].wait_recv()
+        f = ring(cls, 0, 3, half(piece(cls, i2, i1, off(i0, 1)), 0, 1), left)
+        halves.append((e, f))
+    pl.semaphore_wait(near.at[1], 3)
+    tell(2, [core])
+    legs = []
+    far = [[None] * 4 for _ in range(3)]
+
+    def spread_row(cls, d):
+        i2, i1, _ = index[cls]
+        right, left = near_by(cls, 2)
+        ref = row_of(cls, i2, off(i1, d))
+        far[cls][d] = (ring(cls, 2, 2 * d, ref, right), ring(cls, 2, 2 * d + 1, ref, left))
+
+    for cls in range(3):
+        i2, i1, _ = index[cls]
+        for cp in halves[cls]:
+            cp.wait_recv()
+        right, left = near_by(cls, 1)
+        mine = row_of(cls, i2, i1)
+        legs.append((ring(cls, 1, 0, mine, right), ring(cls, 1, 1, mine, left)))
+    for cls in range(3):
+        spread_row(cls, 0)
+    for k in range(2, 5):
+        copies[k].wait()
+    lf = lf_ref[...].astype(F32)
+    zero = jnp.zeros((128, 128), F32)
+    pack(send_f, {0: lf[0:128], 1: lf[128:256], **{r: zero for r in range(2, 8)}})
+    halves = []
+    for cls in range(3):
+        i2, i1, _ = index[cls]
+        right, left = near_by(cls, 1)
+        legs[cls][0].wait_recv()
+        e = ring(cls, 1, 2, half(row_of(cls, i2, off(i1, 3)), 1, 0), right)
+        legs[cls][1].wait_recv()
+        f = ring(cls, 1, 3, half(row_of(cls, i2, off(i1, 1)), 1, 1), left)
+        halves.append((e, f))
+    for cls in range(3):
+        spread_row(cls, 3)
+        spread_row(cls, 1)
+    pl.semaphore_wait(near.at[2], 1)
+    for cls in range(3):
+        for cp in halves[cls]:
+            cp.wait_recv()
+        spread_row(cls, 2)
+    for cls in range(3):
+        cross(cls, index[cls][0], 0)
+    lfx = exchange(send_f, land_f, 0)
+    relays = []
+    for d, k in ((0, 0), (3, 1), (1, 0), (2, 1)):
         for cls in range(3):
-            axis = ORDERS[cls][phase]
-            i = pos[axis]
-            right, left = shifted(pos, axis, 1), shifted(pos, axis, -1)
-            mine = unit(g_ref.at[cls, c], cls, phase, i)
-            a = push(mine, mine, ss.at[cls, phase, 0], rs.at[cls, phase, 0], right)
-            b = push(mine, mine, ss.at[cls, phase, 1], rs.at[cls, phase, 1], left)
-            legs.append((a, b, right, left, i))
-            if phase == 2:
-                cross(cls, i, 0)
-        if phase == 0:
-            copies[1].wait()
-            sel = one_hot(
-                16, 128, lambda r, l: ((r < 2) & (l == r + 126)) | ((r >= 2) & (r < 4) & (l == r - 2))
-            )
-            rows[...] = lax.dot_general(
-                sel, feat_ref[...], dims(1, 1), preferred_element_type=F32
-            ).astype(BF)
-            ha = push(rows, hland.at[0], hs.at[0], hr.at[0], right_shard)
-            hb = push(rows, hland.at[1], hs.at[1], hr.at[1], left_shard)
-            fcp = push(feat_ref, fo_ref, fs, fr, core)
-            pl.semaphore_wait(near.at[0], 3)
-            tell(1, line["y"])
-        if phase == 1:
-            fh[:, 0:128] = feat_ref[...]
-            pl.semaphore_wait(near.at[1], 3)
-            tell(2, [core])
-            for k in range(2, 5):
-                copies[k].wait()
-            lf = lf_ref[...].astype(F32)
-            zero = jnp.zeros((128, 128), F32)
-            pack(send_f, {0: lf[0:128], 1: lf[128:256], **{r: zero for r in range(2, 8)}})
-            ocp = push(og_ref, ogn, os, orr, left_shard)
-            tc = jnp.concatenate([taps_ref[...], jnp.zeros((125, 768), F32)], axis=0)
-            for k in range(6):
-                tcol[k * 128 : (k + 1) * 128, :] = tc[:, k * 128 : (k + 1) * 128].T
-        if phase == 2:
-            pl.semaphore_wait(near.at[2], 1)
-            lfx = exchange(send_f, land_f, 0)
-            ha.wait_recv()
-            hb.wait_recv()
-            row = lax.broadcasted_iota(jnp.int32, (16, 4096), 0)
-            both = jnp.where(row < 2, hland[0].astype(F32), hland[1].astype(F32)).astype(BF)
-            lo = jnp.where(s > 0, 0, 2)
-            hi = jnp.where(s < 127, 4, 2)
-            spread = one_hot(16, 128, lambda r, l: (r == l) & (r >= lo) & (r < hi))
-            fh[:, 128:256] = lax.dot_general(
-                both, spread, dims(0, 0), preferred_element_type=F32
-            ).astype(BF)
-        second = []
-        for cls in range(3):
-            a, b, right, left, i = legs[cls]
-            a.wait_recv()
-            got = half(unit(g_ref.at[cls, c], cls, phase, lax.rem(i + 3, 4)), phase, 0)
-            e = push(got, got, ss.at[cls, phase, 2], rs.at[cls, phase, 2], right)
-            b.wait_recv()
-            got = half(unit(g_ref.at[cls, c], cls, phase, lax.rem(i + 1, 4)), phase, 1)
-            f = push(got, got, ss.at[cls, phase, 3], rs.at[cls, phase, 3], left)
-            second.append((e, f))
-            if phase == 2:
-                cross(cls, lax.rem(i + 3, 4), 1)
-                cross(cls, lax.rem(i + 1, 4), 2)
-        if phase == 2:
-            lfx.wait_recv()
-            unpack(land_f)
-            for ch in range(2):
-                hf[ch] = plane(ch)
-            build_toeplitz(tt0, hf, 0)
-            build_toeplitz(tt1, hf, 1)
-        for cls in range(3):
-            e, f = second[cls]
-            e.wait_recv()
-            f.wait_recv()
-            if phase == 2:
-                cross(cls, lax.rem(legs[cls][4] + 2, 4), 3)
+            i2, i1, _ = index[cls]
+            far[cls][d][k].wait_recv()
+            ref = row_of(cls, off(i2, 1 if k else 3), off(i1, d))
+            relays.append(ring(cls, 2, 8 + d, ref, near_by(cls, 2)[k]))
+    ha = push(rows, hland.at[0], hs.at[0], hr.at[0], right_shard)
+    hb = push(rows, hland.at[1], hs.at[1], hr.at[1], left_shard)
+    for cls in range(3):
+        for d, k in ((0, 1), (3, 0), (1, 1), (2, 0)):
+            far[cls][d][k].wait_recv()
+        cross(cls, off(index[cls][0], 3), 1)
+        cross(cls, off(index[cls][0], 1), 2)
+    fh[:, 0:128] = feat_ref[...]
+    tc = jnp.concatenate([taps_ref[...], jnp.zeros((125, 768), F32)], axis=0)
+    for k in range(6):
+        tcol[k * 128 : (k + 1) * 128, :] = tc[:, k * 128 : (k + 1) * 128].T
+    lfx.wait_recv()
+    unpack(land_f)
+    for ch in range(2):
+        hf[ch] = plane(ch)
+    build_toeplitz(tt0, hf, 0)
+    for cp in relays:
+        cp.wait_recv()
+    for cls in range(3):
+        cross(cls, off(index[cls][0], 2), 3)
+    build_toeplitz(tt1, hf, 1)
+    ha.wait_recv()
+    hb.wait_recv()
+    fcp = push(feat_ref, fo_ref, fs, fr, core)
+    ocp = push(og_ref, ogn, os, orr, left_shard)
+    row = lax.broadcasted_iota(jnp.int32, (16, 4096), 0)
+    both = jnp.where(row < 2, hland[0].astype(F32), hland[1].astype(F32)).astype(BF)
+    lo = jnp.where(s > 0, 0, 2)
+    hi = jnp.where(s < 127, 4, 2)
+    spread = one_hot(16, 128, lambda r, l: (r == l) & (r >= lo) & (r < hi))
+    fh[:, 128:256] = lax.dot_general(both, spread, dims(0, 0), preferred_element_type=F32).astype(BF)
     for cp in d2d:
         cp.wait_recv()
 
@@ -381,6 +423,10 @@
     ret = exchange(send_b, land_b, 2)
     build_toeplitz(tt0, gf, 0)
     build_toeplitz(tt1, gf, 1)
+    for ch in range(2):
+        (y,) = toeplitz_product(tt0 if ch == 0 else tt1, xc.at[ch], 1)
+        rowbuf[pl.ds(ch, 128, stride=8), :] = lax.dot_general(anti, y, dims(1, 1), preferred_element_type=F32)
+    pack(send_c, {})
     ocp.wait_recv()
     ret.wait_recv()
     unpack(land_b)
@@ -393,6 +439,7 @@
     convn = jnp.concatenate([ahead, pltpu.roll(ahead, 126, 1)], axis=0)
     ggn = jnp.concatenate([pltpu.roll(ahead, 124, 1), pltpu.roll(ahead, 122, 1)], axis=0)
     mixed_ref[...] = (feat[0] * conv).astype(BF)
+    store(0, mixed_ref, mixed_hbm)
     ogv = ogn[...].astype(F32)
     last = s == 127
 
@@ -439,6 +486,7 @@
         return total
 
     tcp = tap_send(0, [core], c)
+    fgx = exchange(send_c, land_c, 3)
     fcp.wait_recv()
     pcp.wait_recv()
     for cls in range(3):
@@ -463,8 +511,6 @@
                         k = z * 32 + yl * 16
                         p[cls, i2, i1, i0] = part[k : k + 16, :]
 
-    bufs = {2: (ra3, rb3, rc3, rd3), 1: (ra2, rb2, rc2, rd2), 0: (ra1, rb1, rc1, rd1)}
-
     def add(dst, src):
         dst[...] = (dst[...].astype(F32) + src[...].astype(F32)).astype(BF)
 
@@ -472,73 +518,130 @@
         for q in qs:
             total = None
             for cls in range(3):
-                lhs = jnp.concatenate(
-                    [pd_ref[m * 48 + cls * 16 : m * 48 + cls * 16 + 16, :] for m in range(16)], axis=0
-                )
                 term = lax.dot_general(
-                    lhs, wide_block(g_ref, cls, q // 4, q % 4), dims(0, 0), preferred_element_type=F32
+                    pdt[:, cls * 256 : (cls + 1) * 256], wide_block(g_ref, cls, q // 4, q % 4), dims(1, 0),
+                    preferred_element_type=F32,
                 )
                 total = term if total is None else total + term
             fgrad_ref[q * 512 : (q + 1) * 512, :] = total.T.astype(BF)
 
-    fgx = None
-    for phase in (2, 1, 0):
-        ra, rb, rc, rd = bufs[phase]
-        legs = []
+    def back(cls, phase, k, src, dst, device):
+        return push(src, dst, ss2.at[cls, phase, k], rs2.at[cls, phase, k], device)
+
+    def prow(cls, d2, d1):
+        i2, i1, _ = index[cls]
+        return p.at[cls, off(i2, d2), off(i1, d1)]
+
+    relay = ((2, 1), (0, 3))
+    hops, came = [], []
+    for cls in range(3):
+        hops.append({})
+        came.append({})
+    for j in range(2):
         for cls in range(3):
-            axis = ORDERS[cls][phase]
-            i = pos[axis]
-            right, left = shifted(pos, axis, 1), shifted(pos, axis, -1)
-            far, up, down = (unit(p.at[cls], cls, phase, lax.rem(i + d, 4)) for d in (2, 1, 3))
-            sem = [(ss2.at[cls, phase, k], rs2.at[cls, phase, k]) for k in range(6)]
-            a = push(half(far, phase, 0), ra.at[cls], *sem[0], right)
-            b = push(half(far, phase, 1), rb.at[cls], *sem[1], left)
-            d = push(half(up, phase, 1), half(rc.at[cls], phase, 1), *sem[2], right)
-            e = push(half(down, phase, 0), half(rd.at[cls], phase, 0), *sem[3], left)
-            legs.append((sem, a, b, d, e, up, down, right, left, i))
-        if phase == 2:
-            feat_part(range(2))
-        if phase == 1:
-            feat_part(range(5, 7))
-        if phase == 0:
-            feat_part(range(7, 8))
-        more = []
+            right, left = near_by(cls, 2)
+            hops[cls][0, j] = back(cls, 2, j, prow(cls, 2, relay[j][0]), ra3.at[cls, j], right)
+            hops[cls][1, j] = back(cls, 2, 2 + j, prow(cls, 2, relay[j][1]), rb3.at[cls, j], left)
+    for j in range(2):
         for cls in range(3):
-            sem, a, b, d, e, up, down, right, left, i = legs[cls]
-            a.wait_recv()
-            add(half(up, phase, 0), ra.at[cls])
-            f = push(half(up, phase, 0), half(rc.at[cls], phase, 0), *sem[4], right)
-            b.wait_recv()
-            add(half(down, phase, 1), rb.at[cls])
-            g = push(half(down, phase, 1), half(rd.at[cls], phase, 1), *sem[5], left)
-            more.append((f, g))
-        if phase == 2:
-            tl[1, pos["x"]] = tap_sum(0, tcp, 2)
-            tcp = tap_send(1, line["x"], pos["x"])
-            for ch in range(2):
-                (y,) = toeplitz_product(tt0 if ch == 0 else tt1, xc.at[ch], 1)
-                rowbuf[pl.ds(ch, 128, stride=8), :] = lax.dot_general(
-                    anti, y, dims(1, 1), preferred_element_type=F32
-                )
-            pack(send_c, {})
-            fgx = exchange(send_c, land_c, 3)
-            feat_part(range(2, 5))
-        if phase == 1:
-            tl[2, pos["y"]] = tap_sum(1, tcp, 4)
-            tcp = tap_send(2, line["y"], pos["y"])
-        if phase == 0:
-            tl[3, pos["z"]] = tap_sum(2, tcp, 4)
-            tcp = tap_send(3, line["z"], pos["z"])
+            right, left = near_by(cls, 2)
+            d = relay[j][0]
+            came[cls][1, d] = back(cls, 2, 8 + d, prow(cls, 3, d), rd3.at[cls, d], left)
+            d = relay[j][1]
+            came[cls][0, d] = back(cls, 2, 4 + d, prow(cls, 1, d), rc3.at[cls, d], right)
+    pdt[...] = jnp.concatenate(
+        [
+            pd_ref[m * 48 + cls * 16 : m * 48 + cls * 16 + 16, :].astype(F32)
+            for cls in range(3)
+            for m in range(16)
+        ],
+        axis=0,
+    ).T.astype(BF)
+    feat_part(range(1))
+    for j in range(2):
         for cls in range(3):
-            sem, a, b, d, e, up, down, right, left, i = legs[cls]
-            for k in (d, e) + more[cls]:
-                k.wait_recv()
-            mine = unit(p.at[cls], cls, phase, i)
-            total = mine[...].astype(F32) + rc[cls].astype(F32) + rd[cls].astype(F32)
-            if phase == 0:
-                blk[cls * 16 : (cls + 1) * 16, :] = total
-            else:
-                mine[...] = total.astype(BF)
+            right, left = near_by(cls, 2)
+            d = relay[j][0]
+            hops[cls][0, j].wait_recv()
+            add(prow(cls, 1, d), ra3.at[cls, j])
+            came[cls][0, d] = back(cls, 2, 4 + d, prow(cls, 1, d), rc3.at[cls, d], right)
+            d = relay[j][1]
+            hops[cls][1, j].wait_recv()
+            add(prow(cls, 3, d), rb3.at[cls, j])
+            came[cls][1, d] = back(cls, 2, 8 + d, prow(cls, 3, d), rd3.at[cls, d], left)
+    tl[1, pos["x"]] = tap_sum(0, tcp, 2)
+    tcp = tap_send(1, line["x"], pos["x"])
+    feat_part(range(1, 3))
+
+    def finish_row(cls, d):
+        came[cls][0, d].wait_recv()
+        came[cls][1, d].wait_recv()
+        mine = prow(cls, 0, d)
+        total = mine[...].astype(F32) + rc3[cls, d].astype(F32) + rd3[cls, d].astype(F32)
+        mine[...] = total.astype(BF)
+
+    legs = [{} for _ in range(3)]
+    for cls in range(3):
+        right, left = near_by(cls, 1)
+        finish_row(cls, 2)
+        far_row = prow(cls, 0, 2)
+        legs[cls][0] = back(cls, 1, 0, half(far_row, 1, 0), ra2.at[cls], right)
+        legs[cls][1] = back(cls, 1, 1, half(far_row, 1, 1), rb2.at[cls], left)
+    for cls in range(3):
+        right, left = near_by(cls, 1)
+        finish_row(cls, 1)
+        legs[cls][2] = back(cls, 1, 2, half(prow(cls, 0, 1), 1, 1), half(rc2.at[cls], 1, 1), right)
+        finish_row(cls, 3)
+        legs[cls][3] = back(cls, 1, 3, half(prow(cls, 0, 3), 1, 0), half(rd2.at[cls], 1, 0), left)
+    for cls in range(3):
+        finish_row(cls, 0)
+    for cls in range(3):
+        right, left = near_by(cls, 1)
+        legs[cls][0].wait_recv()
+        add(half(prow(cls, 0, 1), 1, 0), ra2.at[cls])
+        legs[cls][4] = back(cls, 1, 4, half(prow(cls, 0, 1), 1, 0), half(rc2.at[cls], 1, 0), right)
+        legs[cls][1].wait_recv()
+        add(half(prow(cls, 0, 3), 1, 1), rb2.at[cls])
+        legs[cls][5] = back(cls, 1, 5, half(prow(cls, 0, 3), 1, 1), half(rd2.at[cls], 1, 1), left)
+    tl[2, pos["y"]] = tap_sum(1, tcp, 4)
+    tcp = tap_send(2, line["y"], pos["y"])
+    feat_part(range(3, 5))
+    low = [{} for _ in range(3)]
+
+    def part_of(cls, d):
+        i2, i1, i0 = index[cls]
+        return p.at[cls, i2, i1, off(i0, d)]
+
+    for cls in range(3):
+        right, left = near_by(cls, 0)
+        for k in range(2, 6):
+            legs[cls][k].wait_recv()
+        mine = prow(cls, 0, 0)
+        total = mine[...].astype(F32) + rc2[cls].astype(F32) + rd2[cls].astype(F32)
+        mine[...] = total.astype(BF)
+        low[cls][0] = back(cls, 0, 0, half(part_of(cls, 2), 0, 0), ra1.at[cls], right)
+        low[cls][1] = back(cls, 0, 1, half(part_of(cls, 2), 0, 1), rb1.at[cls], left)
+        low[cls][2] = back(cls, 0, 2, half(part_of(cls, 1), 0, 1), half(rc1.at[cls], 0, 1), right)
+        low[cls][3] = back(cls, 0, 3, half(part_of(cls, 3), 0, 0), half(rd1.at[cls], 0, 0), left)
+    tl[3, pos["z"]] = tap_sum(2, tcp, 4)
+    tcp = tap_send(3, line["z"], pos["z"])
+    feat_part(range(5, 7))
+    for cls in range(3):
+        right, left = near_by(cls, 0)
+        low[cls][0].wait_recv()
+        add(half(part_of(cls, 1), 0, 0), ra1.at[cls])
+        low[cls][4] = back(cls, 0, 4, half(part_of(cls, 1), 0, 0), half(rc1.at[cls], 0, 0), right)
+        low[cls][1].wait_recv()
+        add(half(part_of(cls, 3), 0, 1), rb1.at[cls])
+        low[cls][5] = back(cls, 0, 5, half(part_of(cls, 3), 0, 1), half(rd1.at[cls], 0, 1), left)
+    feat_part(range(7, 8))
+    store(1, fgrad_ref, fgrad_hbm)
+    for cls in range(3):
+        for k in range(2, 6):
+            low[cls][k].wait_recv()
+        blk[cls * 16 : (cls + 1) * 16, :] = (
+            part_of(cls, 0)[...].astype(F32) + rc1[cls].astype(F32) + rd1[cls].astype(F32)
+        )
 
     for q in range(8):
         stage2[q, 0:6, :] = blk[q * 6 : (q + 1) * 6, :]
@@ -549,18 +652,22 @@
         final.append(push(stage2.at[q], land2.at[w], s02.at[i], r02.at[i], (n, q)))
     land2[w] = stage2[w]
     tout_ref[...] = tap_sum(3, tcp, 4)[0:3]
+    store(3, tout_ref, tout_hbm)
     fgx.wait_recv()
     unpack(land_c)
     fgout_ref[...] = channels(0).astype(BF)
+    store(2, fgout_ref, fgout_hbm)
     for cp in final:
         cp.wait_recv()
     for q in range(8):
         grad_ref[:, q * 512 : (q + 1) * 512] = land2[q, 0:6, :]
+    store(4, grad_ref, grad_hbm)
     for cp in started:
         cp.wait_send()
-
-
-VM = pl.BlockSpec(memory_space=pltpu.VMEM)
+    for cp in stores:
+        cp.wait()
+
+
 ANY = pl.BlockSpec(memory_space=pl.ANY)
 
 
@@ -578,8 +685,9 @@
             jax.ShapeDtypeStruct((6, 4096), F32),
         ),
         in_specs=[ANY] * 5,
-        out_specs=(VM,) * 5,
+        out_specs=(ANY,) * 5,
         scratch_shapes=[
+            vm((256, 128), BF), vm((4096, 128), BF), vm((256, 128), BF), vm((3, 768), F32), vm((6, 4096), F32), sem((5,)),
             vm((6, 4096), BF), vm((4096, 128), BF), vm((3, 768), F32), vm((256, 128), BF), vm((256, 128), BF),
             vm((8, 8, 512), F32), vm((8, 8, 512), F32), vm((48, 512), F32),
             vm((16, 4096), BF), vm((2, 16, 4096), BF), vm((4096, 256), BF),
@@ -600,11 +708,11 @@
             vm((3, 4, 16, 512), BF), vm((3, 4, 16, 512), BF),
             vm((3, 16, 256), BF), vm((3, 16, 256), BF),
             vm((3, 16, 512), BF), vm((3, 16, 512), BF),
-            vm((8, 8, 512), F32), vm((8, 8, 512), F32), vm((4, 4, 8, 768), F32),
+            vm((8, 8, 512), F32), vm((8, 8, 512), F32), vm((4, 4, 8, 768), F32), vm((128, 768), BF),
             sem((5,)), sem((8,)), sem((8,)),
-            sem((3, 3, 4)), sem((3, 3, 4)), sem((3, 4)), sem((3, 4)),
+            sem((3, 3, 12)), sem((3, 3, 12)), sem((3, 4)), sem((3, 4)),
             sem((2,)), sem((2,)), sem, sem, sem((4,)), sem((4,)), sem, sem,
-            sem, sem, sem((3, 3, 6)), sem((3, 3, 6)), sem((8,)), sem((8,)), sem((4, 3)), sem((4, 3)),
+            sem, sem, sem((3, 3, 12)), sem((3, 3, 12)), sem((8,)), sem((8,)), sem((4, 3)), sem((4, 3)),
             pltpu.SemaphoreType.REGULAR((3,)),
         ],
         compiler_params=pltpu.CompilerParams(
@@ -614,8 +722,33 @@
     )(in_proj, features, taps, out_grad, long_filter)
 
 
+def copy_kernel(*refs):
+    sources, targets, held, (came, left) = refs[:5], refs[5:10], refs[10:15], refs[15:]
+    inward = [pltpu.make_async_copy(sources[k], held[k], came.at[k]) for k in range(5)]
+    outward = [pltpu.make_async_copy(held[k], targets[k], left.at[k]) for k in range(5)]
+    for cp in inward:
+        cp.start()
+    for k in range(5):
+        inward[k].wait()
+        outward[k].start()
+    for cp in outward:
+        cp.wait()
+
+
+def settle(arrays):
+    return pl.pallas_call(
+        copy_kernel,
+        out_shape=tuple(jax.ShapeDtypeStruct(a.shape, a.dtype) for a in arrays),
+        in_specs=[ANY] * 5,
+        out_specs=(ANY,) * 5,
+        scratch_shapes=[pltpu.VMEM(a.shape, a.dtype) for a in arrays]
+        + [pltpu.SemaphoreType.DMA((5,)), pltpu.SemaphoreType.DMA((5,))],
+        name="settle",
+    )(*arrays)
+
+
 def local(features, in_proj, short_taps, long_filter, out_grad):
-    return hyena(in_proj, features, short_taps, out_grad, long_filter)
+    return settle(hyena(in_proj, features, short_taps, out_grad, long_filter))
 
 
 def solution(mesh):

time: 118 us -> 111 us (0.941)
  local copies, waits for them, and re-layouts: 5.66 us -> 0 us
    unnamed x11 -> x0, local copies, waits for them, and re-layouts: 5.66 us -> none
    pallas_call x1, Pallas kernels: 111 us -> 108 us  [hyena(): pl.pallas_call(hyena_kernel, out_shape=(jax.ShapeDtypeStruct((256, 128),...]
    pallas_call x0 -> x1, Pallas kernels: none -> 2.38 us  [settle(): pl.pallas_call(copy_kernel, out_shape=tuple((jax.ShapeDtypeStruct(a.shape...]
where the time goes in v3:
time: 111 us
  Pallas kernels  110 us (99%)
    pallas_call x1, Pallas kernels, hyena(): pl.pallas_call(hyena_kernel, out_shape=(jax.ShapeDtypeStruct((256, 128),...  108 us
    pallas_call x1, Pallas kernels, settle(): pl.pallas_call(copy_kernel, out_shape=tuple((jax.ShapeDtypeStruct(a.shape...  2.38 us

profile of v3, /device:TPU:0, one launch (start us, length us, event | category | flops | bytes accessed | tf_op | source)
XLA Modules:
  0.0 110.9 jit_solution(3704563645976670332)
XLA Ops:
  0.6 107.7 %hyena.1 = (bf16[256,128]{1,0:T(8,128)(2,1)}, bf16[4096,128]{1,0:T(8,128)(2,1)}, bf16[256,128]{1,0:T(8,128)(2,1)}, f32[3,768]{1,0:T(4,128)}, f32[6,4096]{1,0:T(8,128)}) custom-call(bf16[6,4096]{1,0:T(8,128)(2,1)} %proj_hbm.1, bf16[4096,128]{1,0:T(8,128)(2,1)} %feat_hbm.1, f32[3,768]{1,0:T(4,128)} %taps_hbm.1, bf16[256,128]{1,0:T(8,128)(2,1)} %og_hbm.1, ...), custom_call_target="tpu_custom_call" | custom-call | tf_op jit(solution)/shard_map/hyena/pallas_call | solution.py:678
  108.4 2.4 %settle.1 = (bf16[256,128]{1,0:T(8,128)(2,1)}, bf16[4096,128]{1,0:T(8,128)(2,1)}, bf16[256,128]{1,0:T(8,128)(2,1)}, f32[3,768]{1,0:T(4,128)}, f32[6,4096]{1,0:T(8,128)}) custom-call(bf16[256,128]{1,0:T(8,128)(2,1)} %get-tuple-element.10.refs_0_, bf16[4096,128]{1,0:T(8,128)(2,1)} %get-tuple-element.11.refs_1_, bf16[256,128]{1,0:T(8,128)(2,1)} %get-tuple-element.12.refs_2_, ...), custom_call_target="tpu_custom_call" | custom-call | tf_op jit(solution)/shard_map/settle/pallas_call | solution.py:739

commit v4 on v3

--- a/solution.py
+++ b/solution.py
@@ -143,10 +143,10 @@
     stage, land, blk, rows, hland, fh, g_ref, fo_ref, p_ref, halo_ref, tcol,
     rowbuf, send_f, land_f, send_a, land_a, send_b, land_b, send_c, land_c,
     ogn, hf, gf, feat, featn, tt0, tt1, xs, xc, pd_ref,
-    pdo, pdc, p, ra3, rb3, rc3, rd3, ra2, rb2, rc2, rd2, ra1, rb1, rc1, rd1,
+    pdo, pdc, p, ra3, rb3, rc3, rd3, ra2, rb2, rc2, rd2, rz, mid_f, mid_c,
     stage2, land2, tl, pdt,
     ins, s0, r0, ss, rs, ds, dr, hs, hr, fs, fr, xsend, xrecv, os, orr,
-    ps, pr, ss2, rs2, s02, r02, tsn, trc, near,
+    ps, pr, ss2, rs2, s02, r02, tsn, trc, near, xs1, xr1, xs2, xr2,
 ):
     n, w, pos = position()
     c = pos["c"]
@@ -231,10 +231,28 @@
         started.append(cp)
         return cp
 
+    def hand(src, mid, k):
+        cps = []
+        for i in range(1, 8):
+            q = lax.rem(w + i, 8)
+            cps.append(push(src.at[:, q], mid.at[w], xs1.at[k, i], xr1.at[k, i], (n, q)))
+        mid[w] = src[:, w]
+        return cps
+
+    def pass_on(cps, mid, dst, k):
+        for cp in cps:
+            cp.wait_recv()
+        out = []
+        for i in range(1, 16):
+            m = lax.rem(n + i, 16)
+            out.append(push(mid.at[:, m], dst.at[n], xs2.at[k, i], xr2.at[k, i], (m, w)))
+        dst[n] = mid[:, n]
+        return out
+
     def pack(buf, parts):
         for r, value in parts.items():
             rowbuf[pl.ds(r, 128, stride=8), :] = value
-        buf[...] = rowbuf[...].reshape(128, 8, 128).astype(BF)
+        buf[...] = rowbuf[...].reshape(buf.shape).astype(BF)
 
     def unpack(buf):
         rowbuf[...] = buf[...].astype(F32).reshape(1024, 128)
@@ -260,29 +278,11 @@
 
     legs = []
     for cls in range(3):
-        i2, i1, i0 = index[cls]
-        right, left = near_by(cls, 0)
-        mine = piece(cls, i2, i1, i0)
-        legs.append((ring(cls, 0, 0, mine, right), ring(cls, 0, 1, mine, left)))
+        mine = piece(cls, *index[cls])
+        legs.append([ring(cls, 0, d, mine, shifted(pos, ORDERS[cls][0], d)) for d in (1, 2, 3)])
     pl.semaphore_wait(near.at[0], 3)
     tell(1, line["y"])
-    copies[1].wait()
-    sel = one_hot(
-        16, 128, lambda r, l: ((r < 2) & (l == r + 126)) | ((r >= 2) & (r < 4) & (l == r - 2))
-    )
-    rows[...] = lax.dot_general(sel, feat_ref[...], dims(1, 1), preferred_element_type=F32).astype(BF)
-    halves = []
-    for cls in range(3):
-        i2, i1, i0 = index[cls]
-        right, left = near_by(cls, 0)
-        legs[cls][0].wait_recv()
-        e = ring(cls, 0, 2, half(piece(cls, i2, i1, off(i0, 3)), 0, 0), right)
-        legs[cls][1].wait_recv()
-        f = ring(cls, 0, 3, half(piece(cls, i2, i1, off(i0, 1)), 0, 1), left)
-        halves.append((e, f))
-    pl.semaphore_wait(near.at[1], 3)
-    tell(2, [core])
-    legs = []
+    firsts, legs = legs, []
     far = [[None] * 4 for _ in range(3)]
 
     def spread_row(cls, d):
@@ -293,18 +293,20 @@
 
     for cls in range(3):
         i2, i1, _ = index[cls]
-        for cp in halves[cls]:
+        for cp in firsts[cls]:
             cp.wait_recv()
         right, left = near_by(cls, 1)
         mine = row_of(cls, i2, i1)
         legs.append((ring(cls, 1, 0, mine, right), ring(cls, 1, 1, mine, left)))
     for cls in range(3):
         spread_row(cls, 0)
-    for k in range(2, 5):
-        copies[k].wait()
+    pl.semaphore_wait(near.at[1], 3)
+    tell(2, [core])
+    copies[4].wait()
     lf = lf_ref[...].astype(F32)
     zero = jnp.zeros((128, 128), F32)
     pack(send_f, {0: lf[0:128], 1: lf[128:256], **{r: zero for r in range(2, 8)}})
+    lf_half = hand(send_f, mid_f, 0)
     halves = []
     for cls in range(3):
         i2, i1, _ = index[cls]
@@ -324,7 +326,14 @@
         spread_row(cls, 2)
     for cls in range(3):
         cross(cls, index[cls][0], 0)
-    lfx = exchange(send_f, land_f, 0)
+    lfx = pass_on(lf_half, mid_f, land_f, 0)
+    copies[1].wait()
+    sel = one_hot(
+        16, 128, lambda r, l: ((r < 2) & (l == r + 126)) | ((r >= 2) & (r < 4) & (l == r - 2))
+    )
+    rows[...] = lax.dot_general(sel, feat_ref[...], dims(1, 1), preferred_element_type=F32).astype(BF)
+    ha = push(rows, hland.at[0], hs.at[0], hr.at[0], right_shard)
+    hb = push(rows, hland.at[1], hs.at[1], hr.at[1], left_shard)
     relays = []
     for d, k in ((0, 0), (3, 1), (1, 0), (2, 1)):
         for cls in range(3):
@@ -332,37 +341,37 @@
             far[cls][d][k].wait_recv()
             ref = row_of(cls, off(i2, 1 if k else 3), off(i1, d))
             relays.append(ring(cls, 2, 8 + d, ref, near_by(cls, 2)[k]))
-    ha = push(rows, hland.at[0], hs.at[0], hr.at[0], right_shard)
-    hb = push(rows, hland.at[1], hs.at[1], hr.at[1], left_shard)
     for cls in range(3):
         for d, k in ((0, 1), (3, 0), (1, 1), (2, 0)):
             far[cls][d][k].wait_recv()
         cross(cls, off(index[cls][0], 3), 1)
         cross(cls, off(index[cls][0], 1), 2)
     fh[:, 0:128] = feat_ref[...]
+    copies[2].wait()
     tc = jnp.concatenate([taps_ref[...], jnp.zeros((125, 768), F32)], axis=0)
     for k in range(6):
         tcol[k * 128 : (k + 1) * 128, :] = tc[:, k * 128 : (k + 1) * 128].T
-    lfx.wait_recv()
+    for cp in lfx:
+        cp.wait_recv()
     unpack(land_f)
     for ch in range(2):
         hf[ch] = plane(ch)
     build_toeplitz(tt0, hf, 0)
-    for cp in relays:
-        cp.wait_recv()
-    for cls in range(3):
-        cross(cls, off(index[cls][0], 2), 3)
-    build_toeplitz(tt1, hf, 1)
     ha.wait_recv()
     hb.wait_recv()
-    fcp = push(feat_ref, fo_ref, fs, fr, core)
-    ocp = push(og_ref, ogn, os, orr, left_shard)
     row = lax.broadcasted_iota(jnp.int32, (16, 4096), 0)
     both = jnp.where(row < 2, hland[0].astype(F32), hland[1].astype(F32)).astype(BF)
     lo = jnp.where(s > 0, 0, 2)
     hi = jnp.where(s < 127, 4, 2)
     spread = one_hot(16, 128, lambda r, l: (r == l) & (r >= lo) & (r < hi))
     fh[:, 128:256] = lax.dot_general(both, spread, dims(0, 0), preferred_element_type=F32).astype(BF)
+    for cp in relays:
+        cp.wait_recv()
+    for cls in range(3):
+        cross(cls, off(index[cls][0], 2), 3)
+    fcp = push(feat_ref, fo_ref, fs, fr, core)
+    copies[3].wait()
+    ocp = push(og_ref, ogn, os, orr, left_shard)
     for cp in d2d:
         cp.wait_recv()
 
@@ -393,6 +402,7 @@
     cot = og * feat[0]
     pack(send_a, {0: gated[0:128], 1: gated[128:256], 2: cot[0:128], 3: cot[128:256]})
     go = exchange(send_a, land_a, 1)
+    build_toeplitz(tt1, hf, 1)
     go.wait_recv()
     unpack(land_a)
 
@@ -422,11 +432,6 @@
     pack(send_b, {4: ahead})
     ret = exchange(send_b, land_b, 2)
     build_toeplitz(tt0, gf, 0)
-    build_toeplitz(tt1, gf, 1)
-    for ch in range(2):
-        (y,) = toeplitz_product(tt0 if ch == 0 else tt1, xc.at[ch], 1)
-        rowbuf[pl.ds(ch, 128, stride=8), :] = lax.dot_general(anti, y, dims(1, 1), preferred_element_type=F32)
-    pack(send_c, {})
     ocp.wait_recv()
     ret.wait_recv()
     unpack(land_b)
@@ -486,7 +491,6 @@
         return total
 
     tcp = tap_send(0, [core], c)
-    fgx = exchange(send_c, land_c, 3)
     fcp.wait_recv()
     pcp.wait_recv()
     for cls in range(3):
@@ -557,7 +561,7 @@
         ],
         axis=0,
     ).T.astype(BF)
-    feat_part(range(1))
+    build_toeplitz(tt1, gf, 1)
     for j in range(2):
         for cls in range(3):
             right, left = near_by(cls, 2)
@@ -571,7 +575,12 @@
             came[cls][1, d] = back(cls, 2, 8 + d, prow(cls, 3, d), rd3.at[cls, d], left)
     tl[1, pos["x"]] = tap_sum(0, tcp, 2)
     tcp = tap_send(1, line["x"], pos["x"])
-    feat_part(range(1, 3))
+    for ch in range(2):
+        (y,) = toeplitz_product(tt0 if ch == 0 else tt1, xc.at[ch], 1)
+        rowbuf[pl.ds(ch, 128, stride=8), :] = lax.dot_general(anti, y, dims(1, 1), preferred_element_type=F32)
+    pack(send_c, {})
+    fg_half = hand(send_c, mid_c, 1)
+    feat_part(range(2))
 
     def finish_row(cls, d):
         came[cls][0, d].wait_recv()
@@ -605,43 +614,36 @@
         legs[cls][5] = back(cls, 1, 5, half(prow(cls, 0, 3), 1, 1), half(rd2.at[cls], 1, 1), left)
     tl[2, pos["y"]] = tap_sum(1, tcp, 4)
     tcp = tap_send(2, line["y"], pos["y"])
-    feat_part(range(3, 5))
-    low = [{} for _ in range(3)]
+    fgx = pass_on(fg_half, mid_c, land_c, 1)
+    feat_part(range(2, 6))
+    low = []
 
     def part_of(cls, d):
         i2, i1, i0 = index[cls]
         return p.at[cls, i2, i1, off(i0, d)]
 
     for cls in range(3):
-        right, left = near_by(cls, 0)
         for k in range(2, 6):
             legs[cls][k].wait_recv()
         mine = prow(cls, 0, 0)
         total = mine[...].astype(F32) + rc2[cls].astype(F32) + rd2[cls].astype(F32)
         mine[...] = total.astype(BF)
-        low[cls][0] = back(cls, 0, 0, half(part_of(cls, 2), 0, 0), ra1.at[cls], right)
-        low[cls][1] = back(cls, 0, 1, half(part_of(cls, 2), 0, 1), rb1.at[cls], left)
-        low[cls][2] = back(cls, 0, 2, half(part_of(cls, 1), 0, 1), half(rc1.at[cls], 0, 1), right)
-        low[cls][3] = back(cls, 0, 3, half(part_of(cls, 3), 0, 0), half(rd1.at[cls], 0, 0), left)
+        low.append(
+            [
+                back(cls, 0, d, part_of(cls, d), rz.at[cls, d - 1], shifted(pos, ORDERS[cls][0], d))
+                for d in (1, 2, 3)
+            ]
+        )
     tl[3, pos["z"]] = tap_sum(2, tcp, 4)
     tcp = tap_send(3, line["z"], pos["z"])
-    feat_part(range(5, 7))
-    for cls in range(3):
-        right, left = near_by(cls, 0)
-        low[cls][0].wait_recv()
-        add(half(part_of(cls, 1), 0, 0), ra1.at[cls])
-        low[cls][4] = back(cls, 0, 4, half(part_of(cls, 1), 0, 0), half(rc1.at[cls], 0, 0), right)
-        low[cls][1].wait_recv()
-        add(half(part_of(cls, 3), 0, 1), rb1.at[cls])
-        low[cls][5] = back(cls, 0, 5, half(part_of(cls, 3), 0, 1), half(rd1.at[cls], 0, 1), left)
-    feat_part(range(7, 8))
+    feat_part(range(6, 8))
     store(1, fgrad_ref, fgrad_hbm)
     for cls in range(3):
-        for k in range(2, 6):
+        total = part_of(cls, 0)[...].astype(F32)
+        for k in range(3):
             low[cls][k].wait_recv()
-        blk[cls * 16 : (cls + 1) * 16, :] = (
-            part_of(cls, 0)[...].astype(F32) + rc1[cls].astype(F32) + rd1[cls].astype(F32)
-        )
+            total = total + rz[cls, k].astype(F32)
+        blk[cls * 16 : (cls + 1) * 16, :] = total
 
     for q in range(8):
         stage2[q, 0:6, :] = blk[q * 6 : (q + 1) * 6, :]
@@ -653,7 +655,8 @@
     land2[w] = stage2[w]
     tout_ref[...] = tap_sum(3, tcp, 4)[0:3]
     store(3, tout_ref, tout_hbm)
-    fgx.wait_recv()
+    for cp in fgx:
+        cp.wait_recv()
     unpack(land_c)
     fgout_ref[...] = channels(0).astype(BF)
     store(2, fgout_ref, fgout_hbm)
@@ -675,6 +678,7 @@
     sem = pltpu.SemaphoreType.DMA
     vm = pltpu.VMEM
     tile = (128, 8, 128)
+    cut = (16, 8, 8, 128)
     return pl.pallas_call(
         hyena_kernel,
         out_shape=(
@@ -695,7 +699,9 @@
             vm((768, 128), F32), vm((768, 128), F32), vm((768, 128), F32),
             vm((1024, 128), F32),
         ]
-        + [vm(tile, BF)] * 8
+        + [vm(cut, BF)] * 2
+        + [vm(tile, BF)] * 4
+        + [vm(cut, BF)] * 2
         + [
             vm((256, 128), BF), vm((2, 128, 128), F32), vm((2, 128, 128), F32),
             vm((3, 256, 128), F32), vm((3, 256, 128), F32),
@@ -706,14 +712,14 @@
             vm((3, 4, 4, 16, 512), BF), vm((3, 4, 4, 16, 512), BF),
             vm((3, 2, 16, 512), BF), vm((3, 2, 16, 512), BF),
             vm((3, 4, 16, 512), BF), vm((3, 4, 16, 512), BF),
-            vm((3, 16, 256), BF), vm((3, 16, 256), BF),
-            vm((3, 16, 512), BF), vm((3, 16, 512), BF),
+            vm((3, 3, 16, 512), BF), vm((8, 16, 8, 128), BF), vm((8, 16, 8, 128), BF),
             vm((8, 8, 512), F32), vm((8, 8, 512), F32), vm((4, 4, 8, 768), F32), vm((128, 768), BF),
             sem((5,)), sem((8,)), sem((8,)),
             sem((3, 3, 12)), sem((3, 3, 12)), sem((3, 4)), sem((3, 4)),
             sem((2,)), sem((2,)), sem, sem, sem((4,)), sem((4,)), sem, sem,
             sem, sem, sem((3, 3, 12)), sem((3, 3, 12)), sem((8,)), sem((8,)), sem((4, 3)), sem((4, 3)),
             pltpu.SemaphoreType.REGULAR((3,)),
+            sem((2, 8)), sem((2, 8)), sem((2, 16)), sem((2, 16)),
         ],
         compiler_params=pltpu.CompilerParams(
             collective_id=1, has_side_effects=True, vmem_limit_bytes=58 * 1024 * 1024

time: 111 us -> 108 us (0.973)
  Pallas kernels: 110 us -> 107 us
    pallas_call x1, Pallas kernels: 108 us -> 104 us  [hyena(): pl.pallas_call(hyena_kernel, out_shape=(jax.ShapeDtypeStruct((256, 128),...]
where the time goes in v4:
time: 108 us; the launch traced here: 107 us
  Pallas kernels  107 us (99%)
    pallas_call x1, Pallas kernels, hyena(): pl.pallas_call(hyena_kernel, out_shape=(jax.ShapeDtypeStruct((256, 128),...  104 us
    pallas_call x1, Pallas kernels, settle(): pl.pallas_call(copy_kernel, out_shape=tuple((jax.ShapeDtypeStruct(a.shape...  2.38 us

profile of v4, /device:TPU:0, one launch (start us, length us, event | category | flops | bytes accessed | tf_op | source)
XLA Modules:
  0.0 107.4 jit_solution(16023305452807173951)
XLA Ops:
  0.6 104.2 %hyena.1 = (bf16[256,128]{1,0:T(8,128)(2,1)}, bf16[4096,128]{1,0:T(8,128)(2,1)}, bf16[256,128]{1,0:T(8,128)(2,1)}, f32[3,768]{1,0:T(4,128)}, f32[6,4096]{1,0:T(8,128)}) custom-call(bf16[6,4096]{1,0:T(8,128)(2,1)} %proj_hbm.1, bf16[4096,128]{1,0:T(8,128)(2,1)} %feat_hbm.1, f32[3,768]{1,0:T(4,128)} %taps_hbm.1, bf16[256,128]{1,0:T(8,128)(2,1)} %og_hbm.1, ...), custom_call_target="tpu_custom_call" | custom-call | tf_op jit(solution)/shard_map/hyena/pallas_call | solution.py:682
  104.9 2.4 %settle.1 = (bf16[256,128]{1,0:T(8,128)(2,1)}, bf16[4096,128]{1,0:T(8,128)(2,1)}, bf16[256,128]{1,0:T(8,128)(2,1)}, f32[3,768]{1,0:T(4,128)}, f32[6,4096]{1,0:T(8,128)}) custom-call(bf16[256,128]{1,0:T(8,128)(2,1)} %get-tuple-element.10.refs_0_, bf16[4096,128]{1,0:T(8,128)(2,1)} %get-tuple-element.11.refs_1_, bf16[256,128]{1,0:T(8,128)(2,1)} %get-tuple-element.12.refs_2_, ...), custom_call_target="tpu_custom_call" | custom-call | tf_op jit(solution)/shard_map/settle/pallas_call | solution.py:745

commit v5 on v4

--- a/solution.py
+++ b/solution.py
@@ -142,9 +142,9 @@
     proj_ref, feat_ref, taps_ref, og_ref, lf_ref,
     stage, land, blk, rows, hland, fh, g_ref, fo_ref, p_ref, halo_ref, tcol,
     rowbuf, send_f, land_f, send_a, land_a, send_b, land_b, send_c, land_c,
-    ogn, hf, gf, feat, featn, tt0, tt1, xs, xc, pd_ref,
+    ogn, hf, gf, feat, featn, tt, cots, ahead_ref, xs, xc, pd_ref,
     pdo, pdc, p, ra3, rb3, rc3, rd3, ra2, rb2, rc2, rd2, rz, mid_f, mid_c,
-    stage2, land2, tl, pdt,
+    stage2, land2, tl, pdt, rowf, both,
     ins, s0, r0, ss, rs, ds, dr, hs, hr, fs, fr, xsend, xrecv, os, orr,
     ps, pr, ss2, rs2, s02, r02, tsn, trc, near, xs1, xr1, xs2, xr2,
 ):
@@ -282,6 +282,16 @@
         legs.append([ring(cls, 0, d, mine, shifted(pos, ORDERS[cls][0], d)) for d in (1, 2, 3)])
     pl.semaphore_wait(near.at[0], 3)
     tell(1, line["y"])
+    copies[1].wait()
+    sel = one_hot(
+        16, 128, lambda r, l: ((r < 2) & (l == r + 126)) | ((r >= 2) & (r < 4) & (l == r - 2))
+    )
+    edge = lax.dot_general(sel, feat_ref[...], dims(1, 1), preferred_element_type=F32)
+    for k in range(4):
+        for q in range(8):
+            at = (k % 2) * 8 + q
+            rowf[k // 2, at : at + 1, :] = edge[k : k + 1, q * 512 : (q + 1) * 512]
+    rows[...] = rowf[...].astype(BF)
     firsts, legs = legs, []
     far = [[None] * 4 for _ in range(3)]
 
@@ -307,6 +317,8 @@
     zero = jnp.zeros((128, 128), F32)
     pack(send_f, {0: lf[0:128], 1: lf[128:256], **{r: zero for r in range(2, 8)}})
     lf_half = hand(send_f, mid_f, 0)
+    ha = push(rows.at[0], hland.at[0], hs.at[0], hr.at[0], right_shard)
+    hb = push(rows.at[1], hland.at[1], hs.at[1], hr.at[1], left_shard)
     halves = []
     for cls in range(3):
         i2, i1, _ = index[cls]
@@ -327,13 +339,25 @@
     for cls in range(3):
         cross(cls, index[cls][0], 0)
     lfx = pass_on(lf_half, mid_f, land_f, 0)
-    copies[1].wait()
-    sel = one_hot(
-        16, 128, lambda r, l: ((r < 2) & (l == r + 126)) | ((r >= 2) & (r < 4) & (l == r - 2))
-    )
-    rows[...] = lax.dot_general(sel, feat_ref[...], dims(1, 1), preferred_element_type=F32).astype(BF)
-    ha = push(rows, hland.at[0], hs.at[0], hr.at[0], right_shard)
-    hb = push(rows, hland.at[1], hs.at[1], hr.at[1], left_shard)
+    fh[:, 0:128] = feat_ref[...]
+    copies[2].wait()
+    tc = jnp.concatenate([taps_ref[...], jnp.zeros((125, 768), F32)], axis=0)
+    for k in range(6):
+        tcol[k * 128 : (k + 1) * 128, :] = tc[:, k * 128 : (k + 1) * 128].T
+    ha.wait_recv()
+    hb.wait_recv()
+    rowf[...] = hland[...].astype(F32)
+    both[...] = jnp.zeros((16, 4096), F32)
+    for k in range(4):
+        for q in range(8):
+            at = (k % 2) * 8 + q
+            both[k : k + 1, q * 512 : (q + 1) * 512] = rowf[k // 2, at : at + 1, :]
+    lo = jnp.where(s > 0, 0, 2)
+    hi = jnp.where(s < 127, 4, 2)
+    spread = one_hot(16, 128, lambda r, l: (r == l) & (r >= lo) & (r < hi))
+    fh[:, 128:256] = lax.dot_general(
+        both[...].astype(BF), spread, dims(0, 0), preferred_element_type=F32
+    ).astype(BF)
     relays = []
     for d, k in ((0, 0), (3, 1), (1, 0), (2, 1)):
         for cls in range(3):
@@ -346,25 +370,12 @@
             far[cls][d][k].wait_recv()
         cross(cls, off(index[cls][0], 3), 1)
         cross(cls, off(index[cls][0], 1), 2)
-    fh[:, 0:128] = feat_ref[...]
-    copies[2].wait()
-    tc = jnp.concatenate([taps_ref[...], jnp.zeros((125, 768), F32)], axis=0)
-    for k in range(6):
-        tcol[k * 128 : (k + 1) * 128, :] = tc[:, k * 128 : (k + 1) * 128].T
     for cp in lfx:
         cp.wait_recv()
     unpack(land_f)
     for ch in range(2):
         hf[ch] = plane(ch)
-    build_toeplitz(tt0, hf, 0)
-    ha.wait_recv()
-    hb.wait_recv()
-    row = lax.broadcasted_iota(jnp.int32, (16, 4096), 0)
-    both = jnp.where(row < 2, hland[0].astype(F32), hland[1].astype(F32)).astype(BF)
-    lo = jnp.where(s > 0, 0, 2)
-    hi = jnp.where(s < 127, 4, 2)
-    spread = one_hot(16, 128, lambda r, l: (r == l) & (r >= lo) & (r < hi))
-    fh[:, 128:256] = lax.dot_general(both, spread, dims(0, 0), preferred_element_type=F32).astype(BF)
+    build_toeplitz(tt.at[0], hf, 0)
     for cp in relays:
         cp.wait_recv()
     for cls in range(3):
@@ -402,36 +413,39 @@
     cot = og * feat[0]
     pack(send_a, {0: gated[0:128], 1: gated[128:256], 2: cot[0:128], 3: cot[128:256]})
     go = exchange(send_a, land_a, 1)
-    build_toeplitz(tt1, hf, 1)
+    build_toeplitz(tt.at[1], hf, 1)
     go.wait_recv()
     unpack(land_a)
 
     anti = one_hot(128, 128, lambda r, l: r + l == 127)
     row = lax.broadcasted_iota(jnp.int32, (128, 128), 0)
     lane1 = lanes(128)
-    ahead = jnp.zeros((128, 128), F32)
-    cots = []
     for ch in range(2):
         gf[ch] = plane(ch)
-        cots.append(plane(2 + ch).astype(BF))
-    for ch in range(2):
+        cots[ch] = plane(2 + ch).astype(BF)
+    ahead_ref[...] = jnp.zeros((128, 128), F32)
+
+    @pl.loop(0, 2)
+    def _(ch):
         xg = lax.dot_general(anti, gf[ch].astype(BF), dims(1, 1), preferred_element_type=F32)
-        back = lax.dot_general(cots[ch], anti, dims(0, 0), preferred_element_type=F32)
+        back_in = lax.dot_general(cots[ch], anti, dims(0, 0), preferred_element_type=F32)
         spread_blocks(xs, 1, xg)
-        spread_blocks(xs, 0, back)
+        spread_blocks(xs, 0, back_in)
         xc[ch] = xs[:, 0:128]
-        yc, yg = toeplitz_product(tt0 if ch == 0 else tt1, xs, 2)
+        yc, yg = toeplitz_product(tt.at[ch], xs, 2)
         conv = lax.dot_general(yg, anti, dims(0, 0), preferred_element_type=F32)
         gg = lax.dot_general(anti, yc, dims(1, 1), preferred_element_type=F32)
         rowbuf[pl.ds(ch, 128, stride=8), :] = conv
         rowbuf[pl.ds(2 + ch, 128, stride=8), :] = gg
-        for k, value in ((ch, conv), (2 + ch, gg)):
-            nxt = jnp.where(row < 127, pltpu.roll(value, 127, 0), 0.0)
-            moved = pltpu.roll(nxt, 2 * k, 1) if k else nxt
-            ahead = jnp.where((lane1 >= 2 * k) & (lane1 < 2 * k + 2), moved, ahead)
+        for r, value in ((0, conv), (4, gg)):
+            nxt = pltpu.roll(jnp.where(row < 127, pltpu.roll(value, 127, 0), 0.0), r + 2 * ch, 1)
+            keep = (lane1 >= r + 2 * ch) & (lane1 < r + 2 * ch + 2)
+            ahead_ref[...] = jnp.where(keep, nxt, ahead_ref[...])
+
+    ahead = ahead_ref[...]
     pack(send_b, {4: ahead})
     ret = exchange(send_b, land_b, 2)
-    build_toeplitz(tt0, gf, 0)
+    build_toeplitz(tt.at[0], gf, 0)
     ocp.wait_recv()
     ret.wait_recv()
     unpack(land_b)
@@ -501,33 +515,20 @@
                 pdc[to : to + 16, 0:128] = pd_ref[at, :]
                 pdc[to : to + 16, 128:256] = pdo[at, :]
 
-    for yh in range(2):
-        for x in range(4):
-            cols = slice((yh * 4 + x) * 512, (yh * 4 + x + 1) * 512)
-            rhs = jnp.concatenate([feat_ref[cols, :], fo_ref[cols, :]], axis=1)
-            for cls in range(3):
-                part = lax.dot_general(
-                    pdc[cls * 128 : (cls + 1) * 128, :], rhs, dims(1, 1), preferred_element_type=F32
-                ).astype(BF)
-                for z in range(4):
-                    for yl in range(2):
-                        i2, i1, i0 = piece_index(cls, z, yh, yl, x)
-                        k = z * 32 + yl * 16
-                        p[cls, i2, i1, i0] = part[k : k + 16, :]
-
     def add(dst, src):
         dst[...] = (dst[...].astype(F32) + src[...].astype(F32)).astype(BF)
 
     def feat_part(qs):
-        for q in qs:
+        @pl.loop(qs.start, qs.stop)
+        def _(q):
             total = None
             for cls in range(3):
                 term = lax.dot_general(
-                    pdt[:, cls * 256 : (cls + 1) * 256], wide_block(g_ref, cls, q // 4, q % 4), dims(1, 0),
+                    pdt[:, cls * 256 : (cls + 1) * 256], wide_block(g_ref, cls, q // 4, lax.rem(q, 4)), dims(1, 0),
                     preferred_element_type=F32,
                 )
                 total = term if total is None else total + term
-            fgrad_ref[q * 512 : (q + 1) * 512, :] = total.T.astype(BF)
+            fgrad_ref[pl.ds(pl.multiple_of(q * 512, 512), 512), :] = total.T.astype(BF)
 
     def back(cls, phase, k, src, dst, device):
         return push(src, dst, ss2.at[cls, phase, k], rs2.at[cls, phase, k], device)
@@ -541,14 +542,27 @@
     for cls in range(3):
         hops.append({})
         came.append({})
-    for j in range(2):
-        for cls in range(3):
-            right, left = near_by(cls, 2)
+    for cls in range(3):
+
+        @pl.loop(0, 8)
+        def _(q):
+            cols = pl.ds(pl.multiple_of(q * 512, 512), 512)
+            part = lax.dot_general(
+                pdc[cls * 128 : (cls + 1) * 128, :],
+                jnp.concatenate([feat_ref[cols, :], fo_ref[cols, :]], axis=1),
+                dims(1, 1),
+                preferred_element_type=F32,
+            ).astype(BF)
+            for z in range(4):
+                for yl in range(2):
+                    k = z * 32 + yl * 16
+                    i2, i1, i0 = piece_index(cls, z, q // 4, yl, lax.rem(q, 4))
+                    p[cls, i2, i1, i0] = part[k : k + 16, :]
+        right, left = near_by(cls, 2)
+        for j in range(2):
             hops[cls][0, j] = back(cls, 2, j, prow(cls, 2, relay[j][0]), ra3.at[cls, j], right)
             hops[cls][1, j] = back(cls, 2, 2 + j, prow(cls, 2, relay[j][1]), rb3.at[cls, j], left)
-    for j in range(2):
-        for cls in range(3):
-            right, left = near_by(cls, 2)
+        for j in range(2):
             d = relay[j][0]
             came[cls][1, d] = back(cls, 2, 8 + d, prow(cls, 3, d), rd3.at[cls, d], left)
             d = relay[j][1]
@@ -561,7 +575,7 @@
         ],
         axis=0,
     ).T.astype(BF)
-    build_toeplitz(tt1, gf, 1)
+    build_toeplitz(tt.at[1], gf, 1)
     for j in range(2):
         for cls in range(3):
             right, left = near_by(cls, 2)
@@ -575,9 +589,12 @@
             came[cls][1, d] = back(cls, 2, 8 + d, prow(cls, 3, d), rd3.at[cls, d], left)
     tl[1, pos["x"]] = tap_sum(0, tcp, 2)
     tcp = tap_send(1, line["x"], pos["x"])
-    for ch in range(2):
-        (y,) = toeplitz_product(tt0 if ch == 0 else tt1, xc.at[ch], 1)
+
+    @pl.loop(0, 2)
+    def _(ch):
+        (y,) = toeplitz_product(tt.at[ch], xc.at[ch], 1)
         rowbuf[pl.ds(ch, 128, stride=8), :] = lax.dot_general(anti, y, dims(1, 1), preferred_element_type=F32)
+
     pack(send_c, {})
     fg_half = hand(send_c, mid_c, 1)
     feat_part(range(2))
@@ -694,7 +711,7 @@
             vm((256, 128), BF), vm((4096, 128), BF), vm((256, 128), BF), vm((3, 768), F32), vm((6, 4096), F32), sem((5,)),
             vm((6, 4096), BF), vm((4096, 128), BF), vm((3, 768), F32), vm((256, 128), BF), vm((256, 128), BF),
             vm((8, 8, 512), F32), vm((8, 8, 512), F32), vm((48, 512), F32),
-            vm((16, 4096), BF), vm((2, 16, 4096), BF), vm((4096, 256), BF),
+            vm((2, 16, 512), BF), vm((2, 16, 512), BF), vm((4096, 256), BF),
             vm((3, 2, 4, 4, 4, 16, 512), BF), vm((4096, 128), BF),
             vm((768, 128), F32), vm((768, 128), F32), vm((768, 128), F32),
             vm((1024, 128), F32),
@@ -705,7 +722,7 @@
         + [
             vm((256, 128), BF), vm((2, 128, 128), F32), vm((2, 128, 128), F32),
             vm((3, 256, 128), F32), vm((3, 256, 128), F32),
-            vm((1024, 2048), BF), vm((1024, 2048), BF), vm((2048, 256), BF), vm((2, 2048, 128), BF),
+            vm((2, 1024, 2048), BF), vm((2, 128, 128), BF), vm((128, 128), F32), vm((2048, 256), BF), vm((2, 2048, 128), BF),
             vm((768, 128), BF),
             vm((768, 128), BF), vm((384, 256), BF), vm((3, 4, 4, 4, 16, 512), BF),
             vm((3, 2, 4, 16, 512), BF), vm((3, 2, 4, 16, 512), BF),
@@ -713,7 +730,7 @@
             vm((3, 2, 16, 512), BF), vm((3, 2, 16, 512), BF),
             vm((3, 4, 16, 512), BF), vm((3, 4, 16, 512), BF),
             vm((3, 3, 16, 512), BF), vm((8, 16, 8, 128), BF), vm((8, 16, 8, 128), BF),
-            vm((8, 8, 512), F32), vm((8, 8, 512), F32), vm((4, 4, 8, 768), F32), vm((128, 768), BF),
+            vm((8, 8, 512), F32), vm((8, 8, 512), F32), vm((4, 4, 8, 768), F32), vm((128, 768), BF), vm((2, 16, 512), F32), vm((16, 4096), F32),
             sem((5,)), sem((8,)), sem((8,)),
             sem((3, 3, 12)), sem((3, 3, 12)), sem((3, 4)), sem((3, 4)),
             sem((2,)), sem((2,)), sem, sem, sem((4,)), sem((4,)), sem, sem,

time: 108 us -> 104 us (0.963)
  Pallas kernels: 107 us -> 103 us
    pallas_call x1, Pallas kernels: 104 us -> 101 us  [hyena(): pl.pallas_call(hyena_kernel, out_shape=(jax.ShapeDtypeStruct((256, 128),...]
where the time goes in v5:
time: 104 us
  Pallas kernels  103 us (99%)
    pallas_call x1, Pallas kernels, hyena(): pl.pallas_call(hyena_kernel, out_shape=(jax.ShapeDtypeStruct((256, 128),...  101 us
    pallas_call x1, Pallas kernels, settle(): pl.pallas_call(copy_kernel, out_shape=tuple((jax.ShapeDtypeStruct(a.shape...  2.38 us

profile of v5, /device:TPU:0, one launch (start us, length us, event | category | flops | bytes accessed | tf_op | source)
XLA Modules:
  0.0 104.0 jit_solution(2022152467036142652)
XLA Ops:
  0.6 100.8 %hyena.1 = (bf16[256,128]{1,0:T(8,128)(2,1)}, bf16[4096,128]{1,0:T(8,128)(2,1)}, bf16[256,128]{1,0:T(8,128)(2,1)}, f32[3,768]{1,0:T(4,128)}, f32[6,4096]{1,0:T(8,128)}) custom-call(bf16[6,4096]{1,0:T(8,128)(2,1)} %proj_hbm.1, bf16[4096,128]{1,0:T(8,128)(2,1)} %feat_hbm.1, f32[3,768]{1,0:T(4,128)} %taps_hbm.1, bf16[256,128]{1,0:T(8,128)(2,1)} %og_hbm.1, ...), custom_call_target="tpu_custom_call" | custom-call | tf_op jit(solution)/shard_map/hyena/pallas_call | solution.py:699
  101.5 2.4 %settle.1 = (bf16[256,128]{1,0:T(8,128)(2,1)}, bf16[4096,128]{1,0:T(8,128)(2,1)}, bf16[256,128]{1,0:T(8,128)(2,1)}, f32[3,768]{1,0:T(4,128)}, f32[6,4096]{1,0:T(8,128)}) custom-call(bf16[256,128]{1,0:T(8,128)(2,1)} %get-tuple-element.10.refs_0_, bf16[4096,128]{1,0:T(8,128)(2,1)} %get-tuple-element.11.refs_1_, bf16[256,128]{1,0:T(8,128)(2,1)} %get-tuple-element.12.refs_2_, ...), custom_call_target="tpu_custom_call" | custom-call | tf_op jit(solution)/shard_map/settle/pallas_call | solution.py:762

commit v6 on v5

--- a/solution.py
+++ b/solution.py
@@ -143,7 +143,7 @@
     stage, land, blk, rows, hland, fh, g_ref, fo_ref, p_ref, halo_ref, tcol,
     rowbuf, send_f, land_f, send_a, land_a, send_b, land_b, send_c, land_c,
     ogn, hf, gf, feat, featn, tt, cots, ahead_ref, xs, xc, pd_ref,
-    pdo, pdc, p, ra3, rb3, rc3, rd3, ra2, rb2, rc2, rd2, rz, mid_f, mid_c,
+    pdo, pdc, p, ra3, rb3, rc3, rd3, ra2, rb2, rc2, rd2, rz, mid_f, mid_c, turn_f, turn_c, rows_a, rows_b,
     stage2, land2, tl, pdt, rowf, both,
     ins, s0, r0, ss, rs, ds, dr, hs, hr, fs, fr, xsend, xrecv, os, orr,
     ps, pr, ss2, rs2, s02, r02, tsn, trc, near, xs1, xr1, xs2, xr2,
@@ -231,23 +231,41 @@
         started.append(cp)
         return cp
 
+    def deal(value, src):
+        rows_a[...] = value
+        for q in range(8):
+            for r in range(2):
+                rows_b[pl.ds(q * 32 + r, 16, stride=2), :] = rows_a[pl.ds(r * 128 + q, 16, stride=8), :]
+        src[...] = rows_b[...].astype(BF).reshape(8, 32, 128)
+
     def hand(src, mid, k):
         cps = []
         for i in range(1, 8):
             q = lax.rem(w + i, 8)
-            cps.append(push(src.at[:, q], mid.at[w], xs1.at[k, i], xr1.at[k, i], (n, q)))
-        mid[w] = src[:, w]
+            cps.append(push(src.at[q], mid.at[w], xs1.at[k, i], xr1.at[k, i], (n, q)))
+        mid[w] = src[w]
         return cps
 
-    def pass_on(cps, mid, dst, k):
+    def pass_on(cps, mid, turned, dst, k):
         for cp in cps:
             cp.wait_recv()
+        rows_a[...] = mid[...].astype(F32).reshape(256, 128)
+        for q in range(8):
+            for r in range(2):
+                rows_b[pl.ds(q * 2 + r, 16, stride=16), :] = rows_a[pl.ds(q * 32 + r, 16, stride=2), :]
+        turned[...] = rows_b[...].astype(BF).reshape(16, 16, 128)
         out = []
         for i in range(1, 16):
             m = lax.rem(n + i, 16)
-            out.append(push(mid.at[:, m], dst.at[n], xs2.at[k, i], xr2.at[k, i], (m, w)))
-        dst[n] = mid[:, n]
+            out.append(push(turned.at[m], dst.at[n], xs2.at[k, i], xr2.at[k, i], (m, w)))
+        dst[n] = turned[n]
         return out
+
+    def gathered(cps, dst):
+        for cp in cps:
+            cp.wait_recv()
+        rows_a[...] = dst[...].astype(F32).reshape(256, 128)
+        return [rows_a[pl.ds(r, 128, stride=2), :] for r in range(2)]
 
     def pack(buf, parts):
         for r, value in parts.items():
@@ -314,8 +332,8 @@
     tell(2, [core])
     copies[4].wait()
     lf = lf_ref[...].astype(F32)
-    zero = jnp.zeros((128, 128), F32)
-    pack(send_f, {0: lf[0:128], 1: lf[128:256], **{r: zero for r in range(2, 8)}})
+    rowbuf[...] = jnp.zeros((1024, 128), F32)
+    deal(lf, send_f)
     lf_half = hand(send_f, mid_f, 0)
     ha = push(rows.at[0], hland.at[0], hs.at[0], hr.at[0], right_shard)
     hb = push(rows.at[1], hland.at[1], hs.at[1], hr.at[1], left_shard)
@@ -338,7 +356,7 @@
         spread_row(cls, 2)
     for cls in range(3):
         cross(cls, index[cls][0], 0)
-    lfx = pass_on(lf_half, mid_f, land_f, 0)
+    lfx = pass_on(lf_half, mid_f, turn_f, land_f, 0)
     fh[:, 0:128] = feat_ref[...]
     copies[2].wait()
     tc = jnp.concatenate([taps_ref[...], jnp.zeros((125, 768), F32)], axis=0)
@@ -370,11 +388,8 @@
             far[cls][d][k].wait_recv()
         cross(cls, off(index[cls][0], 3), 1)
         cross(cls, off(index[cls][0], 1), 2)
-    for cp in lfx:
-        cp.wait_recv()
-    unpack(land_f)
-    for ch in range(2):
-        hf[ch] = plane(ch)
+    for ch, taps in enumerate(gathered(lfx, land_f)):
+        hf[ch] = taps
     build_toeplitz(tt.at[0], hf, 0)
     for cp in relays:
         cp.wait_recv()
@@ -593,9 +608,9 @@
     @pl.loop(0, 2)
     def _(ch):
         (y,) = toeplitz_product(tt.at[ch], xc.at[ch], 1)
-        rowbuf[pl.ds(ch, 128, stride=8), :] = lax.dot_general(anti, y, dims(1, 1), preferred_element_type=F32)
-
-    pack(send_c, {})
+        hf[ch] = lax.dot_general(anti, y, dims(1, 1), preferred_element_type=F32)
+
+    deal(hf[...].reshape(256, 128), send_c)
     fg_half = hand(send_c, mid_c, 1)
     feat_part(range(2))
 
@@ -631,7 +646,7 @@
         legs[cls][5] = back(cls, 1, 5, half(prow(cls, 0, 3), 1, 1), half(rd2.at[cls], 1, 1), left)
     tl[2, pos["y"]] = tap_sum(1, tcp, 4)
     tcp = tap_send(2, line["y"], pos["y"])
-    fgx = pass_on(fg_half, mid_c, land_c, 1)
+    fgx = pass_on(fg_half, mid_c, turn_c, land_c, 1)
     feat_part(range(2, 6))
     low = []
 
@@ -672,10 +687,7 @@
     land2[w] = stage2[w]
     tout_ref[...] = tap_sum(3, tcp, 4)[0:3]
     store(3, tout_ref, tout_hbm)
-    for cp in fgx:
-        cp.wait_recv()
-    unpack(land_c)
-    fgout_ref[...] = channels(0).astype(BF)
+    fgout_ref[...] = jnp.concatenate(gathered(fgx, land_c), axis=0).astype(BF)
     store(2, fgout_ref, fgout_hbm)
     for cp in final:
         cp.wait_recv()
@@ -695,7 +707,6 @@
     sem = pltpu.SemaphoreType.DMA
     vm = pltpu.VMEM
     tile = (128, 8, 128)
-    cut = (16, 8, 8, 128)
     return pl.pallas_call(
         hyena_kernel,
         out_shape=(
@@ -716,9 +727,9 @@
             vm((768, 128), F32), vm((768, 128), F32), vm((768, 128), F32),
             vm((1024, 128), F32),
         ]
-        + [vm(cut, BF)] * 2
+        + [vm((8, 32, 128), BF), vm((16, 16, 128), BF)]
         + [vm(tile, BF)] * 4
-        + [vm(cut, BF)] * 2
+        + [vm((8, 32, 128), BF), vm((16, 16, 128), BF)]
         + [
             vm((256, 128), BF), vm((2, 128, 128), F32), vm((2, 128, 128), F32),
             vm((3, 256, 128), F32), vm((3, 256, 128), F32),
@@ -729,7 +740,8 @@
             vm((3, 4, 4, 16, 512), BF), vm((3, 4, 4, 16, 512), BF),
             vm((3, 2, 16, 512), BF), vm((3, 2, 16, 512), BF),
             vm((3, 4, 16, 512), BF), vm((3, 4, 16, 512), BF),
-            vm((3, 3, 16, 512), BF), vm((8, 16, 8, 128), BF), vm((8, 16, 8, 128), BF),
+            vm((3, 3, 16, 512), BF), vm((8, 32, 128), BF), vm((8, 32, 128), BF),
+            vm((16, 16, 128), BF), vm((16, 16, 128), BF), vm((256, 128), F32), vm((256, 128), F32),
             vm((8, 8, 512), F32), vm((8, 8, 512), F32), vm((4, 4, 8, 768), F32), vm((128, 768), BF), vm((2, 16, 512), F32), vm((16, 4096), F32),
             sem((5,)), sem((8,)), sem((8,)),
             sem((3, 3, 12)), sem((3, 3, 12)), sem((3, 4)), sem((3, 4)),

time: 104 us -> 100 us (0.962)
  Pallas kernels: 103 us -> 99.1 us
    pallas_call x1, Pallas kernels: 101 us -> 96.8 us  [hyena(): pl.pallas_call(hyena_kernel, out_shape=(jax.ShapeDtypeStruct((256, 128),...]
where the time goes in v6:
time: 100 us; the launch traced here: 99.9 us
  Pallas kernels  99.1 us (99%)
    pallas_call x1, Pallas kernels, hyena(): pl.pallas_call(hyena_kernel, out_shape=(jax.ShapeDtypeStruct((256, 128),...  96.8 us
    pallas_call x1, Pallas kernels, settle(): pl.pallas_call(copy_kernel, out_shape=tuple((jax.ShapeDtypeStruct(a.shape...  2.38 us

profile of v6, /device:TPU:0, one launch (start us, length us, event | category | flops | bytes accessed | tf_op | source)
XLA Modules:
  0.0 99.9 jit_solution(17084648546564117244)
XLA Ops:
  0.6 96.8 %hyena.1 = (bf16[256,128]{1,0:T(8,128)(2,1)}, bf16[4096,128]{1,0:T(8,128)(2,1)}, bf16[256,128]{1,0:T(8,128)(2,1)}, f32[3,768]{1,0:T(4,128)}, f32[6,4096]{1,0:T(8,128)}) custom-call(bf16[6,4096]{1,0:T(8,128)(2,1)} %proj_hbm.1, bf16[4096,128]{1,0:T(8,128)(2,1)} %feat_hbm.1, f32[3,768]{1,0:T(4,128)} %taps_hbm.1, bf16[256,128]{1,0:T(8,128)(2,1)} %og_hbm.1, ...), custom_call_target="tpu_custom_call" | custom-call | tf_op jit(solution)/shard_map/hyena/pallas_call | solution.py:710
  97.4 2.4 %settle.1 = (bf16[256,128]{1,0:T(8,128)(2,1)}, bf16[4096,128]{1,0:T(8,128)(2,1)}, bf16[256,128]{1,0:T(8,128)(2,1)}, f32[3,768]{1,0:T(4,128)}, f32[6,4096]{1,0:T(8,128)}) custom-call(bf16[256,128]{1,0:T(8,128)(2,1)} %get-tuple-element.10.refs_0_, bf16[4096,128]{1,0:T(8,128)(2,1)} %get-tuple-element.11.refs_1_, bf16[256,128]{1,0:T(8,128)(2,1)} %get-tuple-element.12.refs_2_, ...), custom_call_target="tpu_custom_call" | custom-call | tf_op jit(solution)/shard_map/settle/pallas_call | solution.py:774

commit v7 on v6

--- a/solution.py
+++ b/solution.py
@@ -143,7 +143,7 @@
     stage, land, blk, rows, hland, fh, g_ref, fo_ref, p_ref, halo_ref, tcol,
     rowbuf, send_f, land_f, send_a, land_a, send_b, land_b, send_c, land_c,
     ogn, hf, gf, feat, featn, tt, cots, ahead_ref, xs, xc, pd_ref,
-    pdo, pdc, p, ra3, rb3, rc3, rd3, ra2, rb2, rc2, rd2, rz, mid_f, mid_c, turn_f, turn_c, rows_a, rows_b,
+    pdo, pdc, p, ra3, rb3, rc3, rd3, rq, rz, mid_f, mid_c, turn_f, turn_c, rows_a, rows_b,
     stage2, land2, tl, pdt, rowf, both,
     ins, s0, r0, ss, rs, ds, dr, hs, hr, fs, fr, xsend, xrecv, os, orr,
     ps, pr, ss2, rs2, s02, r02, tsn, trc, near, xs1, xr1, xs2, xr2,
@@ -323,9 +323,8 @@
         i2, i1, _ = index[cls]
         for cp in firsts[cls]:
             cp.wait_recv()
-        right, left = near_by(cls, 1)
         mine = row_of(cls, i2, i1)
-        legs.append((ring(cls, 1, 0, mine, right), ring(cls, 1, 1, mine, left)))
+        legs.append([ring(cls, 1, d, mine, shifted(pos, ORDERS[cls][1], d)) for d in (1, 3, 2)])
     for cls in range(3):
         spread_row(cls, 0)
     pl.semaphore_wait(near.at[1], 3)
@@ -337,23 +336,11 @@
     lf_half = hand(send_f, mid_f, 0)
     ha = push(rows.at[0], hland.at[0], hs.at[0], hr.at[0], right_shard)
     hb = push(rows.at[1], hland.at[1], hs.at[1], hr.at[1], left_shard)
-    halves = []
-    for cls in range(3):
-        i2, i1, _ = index[cls]
-        right, left = near_by(cls, 1)
-        legs[cls][0].wait_recv()
-        e = ring(cls, 1, 2, half(row_of(cls, i2, off(i1, 3)), 1, 0), right)
-        legs[cls][1].wait_recv()
-        f = ring(cls, 1, 3, half(row_of(cls, i2, off(i1, 1)), 1, 1), left)
-        halves.append((e, f))
-    for cls in range(3):
-        spread_row(cls, 3)
-        spread_row(cls, 1)
     pl.semaphore_wait(near.at[2], 1)
-    for cls in range(3):
-        for cp in halves[cls]:
-            cp.wait_recv()
-        spread_row(cls, 2)
+    for k, d in ((0, 3), (1, 1), (2, 2)):
+        for cls in range(3):
+            legs[cls][k].wait_recv()
+            spread_row(cls, d)
     for cls in range(3):
         cross(cls, index[cls][0], 0)
     lfx = pass_on(lf_half, mid_f, turn_f, land_f, 0)
@@ -621,29 +608,14 @@
         total = mine[...].astype(F32) + rc3[cls, d].astype(F32) + rd3[cls, d].astype(F32)
         mine[...] = total.astype(BF)
 
-    legs = [{} for _ in range(3)]
-    for cls in range(3):
-        right, left = near_by(cls, 1)
-        finish_row(cls, 2)
-        far_row = prow(cls, 0, 2)
-        legs[cls][0] = back(cls, 1, 0, half(far_row, 1, 0), ra2.at[cls], right)
-        legs[cls][1] = back(cls, 1, 1, half(far_row, 1, 1), rb2.at[cls], left)
-    for cls in range(3):
-        right, left = near_by(cls, 1)
-        finish_row(cls, 1)
-        legs[cls][2] = back(cls, 1, 2, half(prow(cls, 0, 1), 1, 1), half(rc2.at[cls], 1, 1), right)
-        finish_row(cls, 3)
-        legs[cls][3] = back(cls, 1, 3, half(prow(cls, 0, 3), 1, 0), half(rd2.at[cls], 1, 0), left)
+    legs = [[] for _ in range(3)]
+    for d in (2, 1, 3):
+        for cls in range(3):
+            finish_row(cls, d)
+            device = shifted(pos, ORDERS[cls][1], d)
+            legs[cls].append(back(cls, 1, d, prow(cls, 0, d), rq.at[cls, d - 1], device))
     for cls in range(3):
         finish_row(cls, 0)
-    for cls in range(3):
-        right, left = near_by(cls, 1)
-        legs[cls][0].wait_recv()
-        add(half(prow(cls, 0, 1), 1, 0), ra2.at[cls])
-        legs[cls][4] = back(cls, 1, 4, half(prow(cls, 0, 1), 1, 0), half(rc2.at[cls], 1, 0), right)
-        legs[cls][1].wait_recv()
-        add(half(prow(cls, 0, 3), 1, 1), rb2.at[cls])
-        legs[cls][5] = back(cls, 1, 5, half(prow(cls, 0, 3), 1, 1), half(rd2.at[cls], 1, 1), left)
     tl[2, pos["y"]] = tap_sum(1, tcp, 4)
     tcp = tap_send(2, line["y"], pos["y"])
     fgx = pass_on(fg_half, mid_c, turn_c, land_c, 1)
@@ -655,10 +627,12 @@
         return p.at[cls, i2, i1, off(i0, d)]
 
     for cls in range(3):
-        for k in range(2, 6):
-            legs[cls][k].wait_recv()
         mine = prow(cls, 0, 0)
-        total = mine[...].astype(F32) + rc2[cls].astype(F32) + rd2[cls].astype(F32)
+        total = mine[...].astype(F32)
+        for cp in legs[cls]:
+            cp.wait_recv()
+        for k in range(3):
+            total = total + rq[cls, k].astype(F32)
         mine[...] = total.astype(BF)
         low.append(
             [
@@ -738,8 +712,7 @@
             vm((768, 128), BF), vm((384, 256), BF), vm((3, 4, 4, 4, 16, 512), BF),
             vm((3, 2, 4, 16, 512), BF), vm((3, 2, 4, 16, 512), BF),
             vm((3, 4, 4, 16, 512), BF), vm((3, 4, 4, 16, 512), BF),
-            vm((3, 2, 16, 512), BF), vm((3, 2, 16, 512), BF),
-            vm((3, 4, 16, 512), BF), vm((3, 4, 16, 512), BF),
+            vm((3, 3, 4, 16, 512), BF),
             vm((3, 3, 16, 512), BF), vm((8, 32, 128), BF), vm((8, 32, 128), BF),
             vm((16, 16, 128), BF), vm((16, 16, 128), BF), vm((256, 128), F32), vm((256, 128), F32),
             vm((8, 8, 512), F32), vm((8, 8, 512), F32), vm((4, 4, 8, 768), F32), vm((128, 768), BF), vm((2, 16, 512), F32), vm((16, 4096), F32),

time: 100 us -> 99.1 us (level)
  no operation moved by 1% of the time
where the time goes in v7:
time: 99.1 us; the launch traced here: 99 us
  Pallas kernels  98.2 us (99%)
    pallas_call x1, Pallas kernels, hyena(): pl.pallas_call(hyena_kernel, out_shape=(jax.ShapeDtypeStruct((256, 128),...  95.8 us
    pallas_call x1, Pallas kernels, settle(): pl.pallas_call(copy_kernel, out_shape=tuple((jax.ShapeDtypeStruct(a.shape...  2.38 us

profile of v7, /device:TPU:0, one launch (start us, length us, event | category | flops | bytes accessed | tf_op | source)
XLA Modules:
  0.0 99.0 jit_solution(11348205838668572326)
XLA Ops:
  0.6 95.8 %hyena.1 = (bf16[256,128]{1,0:T(8,128)(2,1)}, bf16[4096,128]{1,0:T(8,128)(2,1)}, bf16[256,128]{1,0:T(8,128)(2,1)}, f32[3,768]{1,0:T(4,128)}, f32[6,4096]{1,0:T(8,128)}) custom-call(bf16[6,4096]{1,0:T(8,128)(2,1)} %proj_hbm.1, bf16[4096,128]{1,0:T(8,128)(2,1)} %feat_hbm.1, f32[3,768]{1,0:T(4,128)} %taps_hbm.1, bf16[256,128]{1,0:T(8,128)(2,1)} %og_hbm.1, ...), custom_call_target="tpu_custom_call" | custom-call | tf_op jit(solution)/shard_map/hyena/pallas_call | solution.py:684
  96.4 2.4 %settle.1 = (bf16[256,128]{1,0:T(8,128)(2,1)}, bf16[4096,128]{1,0:T(8,128)(2,1)}, bf16[256,128]{1,0:T(8,128)(2,1)}, f32[3,768]{1,0:T(4,128)}, f32[6,4096]{1,0:T(8,128)}) custom-call(bf16[256,128]{1,0:T(8,128)(2,1)} %get-tuple-element.10.refs_0_, bf16[4096,128]{1,0:T(8,128)(2,1)} %get-tuple-element.11.refs_1_, bf16[256,128]{1,0:T(8,128)(2,1)} %get-tuple-element.12.refs_2_, ...), custom_call_target="tpu_custom_call" | custom-call | tf_op jit(solution)/shard_map/settle/pallas_call | solution.py:747

commit v8 on v7

--- a/solution.py
+++ b/solution.py
@@ -732,13 +732,16 @@
 
 def copy_kernel(*refs):
     sources, targets, held, (came, left) = refs[:5], refs[5:10], refs[10:15], refs[15:]
-    inward = [pltpu.make_async_copy(sources[k], held[k], came.at[k]) for k in range(5)]
-    outward = [pltpu.make_async_copy(held[k], targets[k], left.at[k]) for k in range(5)]
+    spans = [(1, pl.ds(1024 * i, 1024)) for i in range(4)] + [(k, slice(None)) for k in (0, 2, 3, 4)]
+    inward, outward = [], []
+    for i, (k, at) in enumerate(spans):
+        inward.append(pltpu.make_async_copy(sources[k].at[at], held[k].at[at], came.at[i]))
+        outward.append(pltpu.make_async_copy(held[k].at[at], targets[k].at[at], left.at[i]))
     for cp in inward:
         cp.start()
-    for k in range(5):
-        inward[k].wait()
-        outward[k].start()
+    for i in range(8):
+        inward[i].wait()
+        outward[i].start()
     for cp in outward:
         cp.wait()
 
@@ -750,7 +753,7 @@
         in_specs=[ANY] * 5,
         out_specs=(ANY,) * 5,
         scratch_shapes=[pltpu.VMEM(a.shape, a.dtype) for a in arrays]
-        + [pltpu.SemaphoreType.DMA((5,)), pltpu.SemaphoreType.DMA((5,))],
+        + [pltpu.SemaphoreType.DMA((8,)), pltpu.SemaphoreType.DMA((8,))],
         name="settle",
     )(*arrays)
 

time: 99.1 us -> 98.9 us (level)
  no operation moved by 1% of the time
where the time goes in v8:
time: 98.9 us; the launch traced here: 98.7 us
  Pallas kernels  97.9 us (99%)
    pallas_call x1, Pallas kernels, hyena(): pl.pallas_call(hyena_kernel, out_shape=(jax.ShapeDtypeStruct((256, 128),...  95.8 us
    pallas_call x1, Pallas kernels, settle(): pl.pallas_call(copy_kernel, out_shape=tuple((jax.ShapeDtypeStruct(a.shape...  2.14 us

profile of v8, /device:TPU:0, one launch (start us, length us, event | category | flops | bytes accessed | tf_op | source)
XLA Modules:
  0.0 98.7 jit_solution(12622158992366676745)
XLA Ops:
  0.6 95.8 %hyena.1 = (bf16[256,128]{1,0:T(8,128)(2,1)}, bf16[4096,128]{1,0:T(8,128)(2,1)}, bf16[256,128]{1,0:T(8,128)(2,1)}, f32[3,768]{1,0:T(4,128)}, f32[6,4096]{1,0:T(8,128)}) custom-call(bf16[6,4096]{1,0:T(8,128)(2,1)} %proj_hbm.1, bf16[4096,128]{1,0:T(8,128)(2,1)} %feat_hbm.1, f32[3,768]{1,0:T(4,128)} %taps_hbm.1, bf16[256,128]{1,0:T(8,128)(2,1)} %og_hbm.1, ...), custom_call_target="tpu_custom_call" | custom-call | tf_op jit(solution)/shard_map/hyena/pallas_call | solution.py:684
  96.4 2.1 %settle.1 = (bf16[256,128]{1,0:T(8,128)(2,1)}, bf16[4096,128]{1,0:T(8,128)(2,1)}, bf16[256,128]{1,0:T(8,128)(2,1)}, f32[3,768]{1,0:T(4,128)}, f32[6,4096]{1,0:T(8,128)}) custom-call(bf16[256,128]{1,0:T(8,128)(2,1)} %get-tuple-element.10.refs_0_, bf16[4096,128]{1,0:T(8,128)(2,1)} %get-tuple-element.11.refs_1_, bf16[256,128]{1,0:T(8,128)(2,1)} %get-tuple-element.12.refs_2_, ...), custom_call_target="tpu_custom_call" | custom-call | tf_op jit(solution)/shard_map/settle/pallas_call | solution.py:750
